TPU v7x, 32 devices: a whole 2x2x4 slice. The times are simulated.
32 devices in a mesh: stream: 8 (over y, x, core), blk: 4 (over z).
Axes of the slice: x: 2, y: 2, z: 4, core: 2. Of those that a mesh axis runs over, the one named last changes fastest.
Arguments:
- segment: bfloat16 [8, 512, 1024], P('stream', 'blk'), may hold values from -6 to 6
- memory: bfloat16 [8, 512, 1024], P('stream', 'blk'), may hold values from -6 to 6
- compressed: bfloat16 [8, 512, 1024], P('stream', 'blk'), may hold values from -6 to 6
- document_labels: int32 [8, 3, 512], P('stream'), may hold values from 0 to 3, as said below
- memory_filled_count: int32 [8], P('stream'), may hold values from 0 to 1024, as said below
- norm_gain: float32 [1024], replicated, may hold values from 0.1 to 1.9
- w_query: bfloat16 [1024, 1024], replicated, may hold values from -0.1875 to 0.1875
- w_key: bfloat16 [1024, 1024], replicated, may hold values from -0.1875 to 0.1875
- w_value: bfloat16 [1024, 1024], replicated, may hold values from -0.1875 to 0.1875
- w_output: bfloat16 [1024, 1024], replicated, may hold values from -0.75 to 0.75
- ffn_gain: float32 [1024], replicated, may hold values from 0.1 to 1.9
- w_expand: bfloat16 [1024, 4096], replicated, may hold values from -0.1875 to 0.1875
- w_reduce: bfloat16 [4096, 1024], replicated, may hold values from -0.1875 to 0.1875
- w_compress: bfloat16 [2048, 1024], replicated, may hold values from -0.125 to 0.125
- result_cotangent: bfloat16 [8, 512, 1024], P('stream', 'blk'), may hold values from -6 to 6
- compressed_cotangent: bfloat16 [8, 256, 1024], P('stream', 'blk'), may hold values from -6 to 6
Outputs:
- result: bfloat16 [8, 512, 1024], P('stream', 'blk')
- new_compressed: bfloat16 [8, 256, 1024], P('stream', 'blk')
- grad_segment: bfloat16 [8, 512, 1024], P('stream', 'blk')
- grad_norm_gain: float32 [1024], P(('stream', 'blk'))
- grad_query: float32 [1024, 1024], P(('stream', 'blk'))
- grad_key: float32 [1024, 1024], P(('stream', 'blk'))
- grad_value: float32 [1024, 1024], P(('stream', 'blk'))
- grad_output: float32 [1024, 1024], P(('stream', 'blk'))
- grad_ffn_gain: float32 [1024], P(('stream', 'blk'))
- grad_expand: float32 [1024, 4096], P(('stream', 'blk'))
- grad_reduce: float32 [4096, 1024], P(None, ('stream', 'blk'))
- grad_compress: float32 [2048, 1024], P(('stream', 'blk'))
Inputs may be any that keep to these rules, and one draw needn't show every extreme that they name: `document_labels`: per stream the ids never fall along the compressed slots, then the memory slots, then the segment positions. `memory_filled_count`: counts the most recent slots of compressed memory and memory taken together.
All inputs are finite; a program needn't handle non-finite values.
Results may differ from a plain program's by a relative error of at most 0.014.
Values may be sent and summed in bfloat16 or wider, within the bound.
No kernel may reach another device: no remote copies, remote signals or barrier semaphores. Data moves between devices by JAX's collectives and lax.ppermute only.
A program may use at most 256 MiB of HBM per device.

v0:
```python
import jax
import jax.numpy as jnp
from jax import lax
from jax.sharding import PartitionSpec as P

HD = 128
RATE = 2


epsilon = 1e-05
masked_score = -1e30


def layer_norm(rows_in, gain):
    center = jnp.mean(rows_in, axis=-1, keepdims=True)
    offset = rows_in - center
    spread = jnp.mean(offset * offset, axis=-1, keepdims=True)
    return offset * lax.rsqrt(spread + epsilon) * gain


def exact_gelu(values_in):
    return jax.nn.gelu(values_in, approximate=False)


def on_device(
    segment,
    memory,
    compressed,
    document_labels,
    memory_filled_count,
    norm_gain,
    w_query,
    w_key,
    w_value,
    w_output,
    ffn_gain,
    w_expand,
    w_reduce,
    w_compress,
    result_cotangent,
    compressed_cotangent,
):
    streams, block_rows, model_width = segment.shape
    head_count = model_width // HD
    blocks = lax.axis_size("blk")
    my_block = lax.axis_index("blk")
    seg_len = block_rows * blocks
    key_count = 3 * seg_len
    score_scale = HD ** (-0.5)
    stacked = jnp.concatenate([compressed, memory, segment], axis=1).astype(jnp.float32)
    normed_full, norm_pull = jax.vjp(layer_norm, stacked, norm_gain)
    normed = normed_full.astype(jnp.bfloat16)
    seg_normed = normed[:, 2 * block_rows :]
    queries = jnp.einsum(
        "srd,de->sre", seg_normed, w_query, preferred_element_type=jnp.float32
    ).astype(jnp.bfloat16)
    query_heads = queries.reshape(streams, block_rows, head_count, HD)
    keys = jnp.einsum("srd,de->rse", normed, w_key, preferred_element_type=jnp.float32).astype(
        jnp.bfloat16
    )
    values = jnp.einsum("srd,de->rse", normed, w_value, preferred_element_type=jnp.float32).astype(
        jnp.bfloat16
    )
    all_keys, all_values = (
        lax.all_gather(keys, "blk", axis=0, tiled=True),
        lax.all_gather(values, "blk", axis=0, tiled=True),
    )
    key_index = jnp.arange(key_count, dtype=jnp.int32)
    key_owner = key_index // (3 * block_rows)
    within = key_index % (3 * block_rows)
    key_kind = within // block_rows
    key_pos = key_owner * block_rows + within % block_rows
    key_slot = key_kind * seg_len + key_pos
    key_docs = (
        document_labels.reshape(streams, 3, blocks, block_rows)
        .transpose(0, 2, 1, 3)
        .reshape(streams, key_count)
    )
    query_pos = my_block * block_rows + jnp.arange(block_rows, dtype=jnp.int32)
    query_docs = lax.dynamic_slice_in_dim(
        document_labels[:, 2], my_block * block_rows, block_rows, 1
    )
    in_memory = key_slot[None, :] >= 2 * seg_len - memory_filled_count[:, None]
    causal = key_pos[None, :] <= query_pos[:, None]
    visible = jnp.where((key_kind < 2)[None, None, :], in_memory[:, None, :], causal[None, :, :])
    allowed = visible & (key_docs[:, None, :] == query_docs[:, :, None])

    def scores_of(key_set):
        key_view = key_set.reshape(key_count, streams, head_count, HD)
        raw_scores = (
            jnp.einsum("sqhd,kshd->shqk", query_heads, key_view, preferred_element_type=jnp.float32)
            * score_scale
        )
        return jnp.where(allowed[:, None], raw_scores, masked_score)

    scores = scores_of(all_keys)
    row_top = jnp.max(scores, axis=-1, keepdims=True)
    weights = jnp.exp(scores - row_top)
    row_total = jnp.sum(weights, axis=-1, keepdims=True)
    probs = (weights / row_total).astype(jnp.bfloat16)
    log_total = row_top + jnp.log(row_total)
    value_heads = all_values.reshape(key_count, streams, head_count, HD)
    attended = jnp.einsum("shqk,kshd->sqhd", probs, value_heads, preferred_element_type=jnp.float32)
    attended = attended.reshape(streams, block_rows, model_width).astype(jnp.bfloat16)
    middle = segment.astype(jnp.float32) + jnp.einsum(
        "sre,ed->srd", attended, w_output, preferred_element_type=jnp.float32
    )
    normed_ffn_full, ffn_pull = jax.vjp(layer_norm, middle, ffn_gain)
    normed_ffn = normed_ffn_full.astype(jnp.bfloat16)
    hidden = jnp.einsum("srd,df->srf", normed_ffn, w_expand, preferred_element_type=jnp.float32)
    activated_full, gelu_pull = jax.vjp(exact_gelu, hidden)
    activated = activated_full.astype(jnp.bfloat16)
    result = (
        middle + jnp.einsum("srf,fd->srd", activated, w_reduce, preferred_element_type=jnp.float32)
    ).astype(jnp.bfloat16)
    mem_pairs = memory.reshape(streams, block_rows // RATE, RATE * model_width)
    new_compressed = jnp.einsum(
        "srp,pd->srd", mem_pairs, w_compress, preferred_element_type=jnp.float32
    ).astype(jnp.bfloat16)
    reduce_turned = jnp.einsum(
        "srd,srf->df", result_cotangent, activated, preferred_element_type=jnp.float32
    )
    d_activated = jnp.einsum(
        "srd,fd->srf", result_cotangent, w_reduce, preferred_element_type=jnp.float32
    )
    d_hidden = gelu_pull(d_activated)[0].astype(jnp.bfloat16)
    grad_expand = jnp.einsum(
        "srd,srf->df", normed_ffn, d_hidden, preferred_element_type=jnp.float32
    )
    d_normed_ffn = jnp.einsum("srf,df->srd", d_hidden, w_expand, preferred_element_type=jnp.float32)
    d_middle_norm, grad_ffn_gain = ffn_pull(d_normed_ffn)
    d_middle = result_cotangent.astype(jnp.float32) + d_middle_norm
    d_branch = d_middle.astype(jnp.bfloat16)
    grad_output = jnp.einsum("sre,srd->ed", attended, d_branch, preferred_element_type=jnp.float32)
    d_attended = jnp.einsum(
        "srd,ed->sre", d_branch, w_output, preferred_element_type=jnp.float32
    ).astype(jnp.bfloat16)
    d_attended = d_attended.reshape(streams, block_rows, head_count, HD)
    key_heads = all_keys.reshape(key_count, streams, head_count, HD)
    probs_full = jnp.exp(scores_of(all_keys) - log_total)
    probs_low = probs_full.astype(jnp.bfloat16)
    d_probs = jnp.einsum(
        "sqhd,kshd->shqk", d_attended, value_heads, preferred_element_type=jnp.float32
    )
    row_delta = jnp.sum(probs_full * d_probs, axis=-1, keepdims=True)
    d_scores = (probs_full * (d_probs - row_delta)).astype(jnp.bfloat16)
    d_queries = (
        jnp.einsum("shqk,kshd->sqhd", d_scores, key_heads, preferred_element_type=jnp.float32)
        * score_scale
    )
    d_queries = d_queries.astype(jnp.bfloat16).reshape(streams, block_rows, model_width)
    count = 3 * block_rows * lax.axis_size("blk")
    key_part = (
        jnp.einsum("shqk,sqhd->kshd", d_scores, query_heads, preferred_element_type=jnp.float32)
        * score_scale
    )
    value_part = jnp.einsum(
        "shqk,sqhd->kshd", probs_low, d_attended, preferred_element_type=jnp.float32
    )
    key_grads = lax.psum_scatter(
        jnp.stack(
            [
                key_part.reshape(count, streams, model_width),
                value_part.reshape(count, streams, model_width),
            ],
            axis=1,
        ).astype(jnp.bfloat16),
        "blk",
        scatter_dimension=0,
        tiled=True,
    ).astype(jnp.float32)
    d_keys = key_grads[:, 0].astype(jnp.bfloat16)
    d_values = key_grads[:, 1].astype(jnp.bfloat16)
    grad_query = jnp.einsum(
        "srd,sre->de", seg_normed, d_queries, preferred_element_type=jnp.float32
    )
    grad_key = jnp.einsum("srd,rse->de", normed, d_keys, preferred_element_type=jnp.float32)
    grad_value = jnp.einsum("srd,rse->de", normed, d_values, preferred_element_type=jnp.float32)
    d_normed = jnp.einsum("rse,de->srd", d_keys, w_key, preferred_element_type=jnp.float32)
    d_normed = d_normed + jnp.einsum(
        "rse,de->srd", d_values, w_value, preferred_element_type=jnp.float32
    )
    d_seg_normed = jnp.einsum("sre,de->srd", d_queries, w_query, preferred_element_type=jnp.float32)
    d_normed = d_normed + jnp.pad(d_seg_normed, ((0, 0), (2 * block_rows, 0), (0, 0)))
    d_stacked, grad_norm_gain = norm_pull(d_normed)
    grad_segment = (d_middle + d_stacked[:, 2 * block_rows :]).astype(jnp.bfloat16)
    grad_compress = jnp.einsum(
        "srp,srd->pd", mem_pairs, compressed_cotangent, preferred_element_type=jnp.float32
    )
    weight_grads = (
        grad_norm_gain,
        grad_query,
        grad_key,
        grad_value,
        grad_output,
        grad_ffn_gain,
        grad_expand,
        reduce_turned,
        grad_compress,
    )
    summed = (
        lax.psum_scatter(weight_grads[0], ("stream", "blk"), scatter_dimension=0, tiled=True),
        lax.psum_scatter(weight_grads[1], ("stream", "blk"), scatter_dimension=0, tiled=True),
        lax.psum_scatter(weight_grads[2], ("stream", "blk"), scatter_dimension=0, tiled=True),
        lax.psum_scatter(weight_grads[3], ("stream", "blk"), scatter_dimension=0, tiled=True),
        lax.psum_scatter(weight_grads[4], ("stream", "blk"), scatter_dimension=0, tiled=True),
        lax.psum_scatter(weight_grads[5], ("stream", "blk"), scatter_dimension=0, tiled=True),
        lax.psum_scatter(weight_grads[6], ("stream", "blk"), scatter_dimension=0, tiled=True),
        lax.psum_scatter(weight_grads[7], ("stream", "blk"), scatter_dimension=0, tiled=True),
        lax.psum_scatter(weight_grads[8], ("stream", "blk"), scatter_dimension=0, tiled=True),
    )
    grad_reduce = summed[7].T
    return (
        result,
        new_compressed,
        grad_segment,
        summed[0],
        summed[1],
        summed[2],
        summed[3],
        summed[4],
        summed[5],
        summed[6],
        grad_reduce,
        summed[8],
    )


def solution(mesh):
    in_specs = (
        P("stream", "blk", None),
        P("stream", "blk", None),
        P("stream", "blk", None),
        P("stream", None, None),
        P("stream"),
        P(),
        P(),
        P(),
        P(),
        P(),
        P(),
        P(),
        P(),
        P(),
        P("stream", "blk", None),
        P("stream", "blk", None),
    )
    out_specs = (
        P("stream", "blk", None),
        P("stream", "blk", None),
        P("stream", "blk", None),
        P(("stream", "blk")),
        P(("stream", "blk"), None),
        P(("stream", "blk"), None),
        P(("stream", "blk"), None),
        P(("stream", "blk"), None),
        P(("stream", "blk")),
        P(("stream", "blk"), None),
        P(None, ("stream", "blk")),
        P(("stream", "blk"), None),
    )
    return jax.shard_map(
        on_device, mesh=mesh, in_specs=in_specs, out_specs=out_specs, check_vma=False
    )
```

profile of v0, /device:TPU:0, one launch (start us, length us, event | category | flops | bytes accessed | tf_op | source)
XLA Modules:
  0.0 1838.5 jit_solution(13318125017227896524)
XLA Ops:
  13.4 3.5 fusion.21
  21.0 58.7 %all-gather.3.cloned.1.call-done = bf16[1536,1,1024]{2,0,1:T(8,128)(2,1)} async-done(((bf16[384,1,1024]{2,0,1:T(8,128)(2,1)}), bf16[1536,1,1024]{2,0,1:T(8,128)(2,1)}) %all-gather.3.cloned.1.call-update) | async-done | bytes 3145744 | tf_op jit(solution)/shard_map/all_gather | solution.py:66
  79.7 4.4 copy.67
  84.1 59.3 %all-gather.5.cloned.1.call-done = bf16[1536,1,1024]{2,0,1:T(8,128)(2,1)} async-done(((bf16[384,1,1024]{2,0,1:T(8,128)(2,1)}), bf16[1536,1,1024]{2,0,1:T(8,128)(2,1)}) %all-gather.5.cloned.1.call-update) | async-done | bytes 3145744 | tf_op jit(solution)/shard_map/all_gather | solution.py:65
  143.4 4.7 copy.65
  161.7 7.6 add_convert_fusion
  169.4 3.5 fusion.35
  178.2 6.0 multiply_reduce_fusion
  184.2 3.9 convolution_convert_fusion
  188.1 3.7 multiply_convert_fusion.1
  196.5 8.8 copy.61
  205.4 3.8 fusion.28
  209.9 3.9 fusion.55
  213.8 3.7 fusion.78
  218.4 5.5 fusion.53
  224.0 90.9 %reduce-scatter.25.cloned.1.call-done = bf16[384,2048]{1,0:T(8,128)(2,1)} async-done(((bf16[1536,2048]{1,0:T(8,128)(2,1)}), bf16[384,2048]{1,0:T(8,128)(2,1)}) %reduce-scatter.25.cloned.1.call-update) | async-done | bytes 1572880
  314.9 13.6 copy.62
  328.4 4.6 fusion.41
  333.1 4.6 fusion.38
  338.4 9.4 fusion.70
  347.9 11.0 convolution_bitcast_fusion
  358.9 17.5 copy.59
  376.4 3.9 fusion.29
  382.0 8.8 fusion.24
  395.0 41.4 %all-reduce.3 = (f32[1024]{0:T(1024)S(1)}, f32[1024]{0:T(1024)S(1)}) all-reduce(f32[1024]{0:T(1024)S(1)} %get-tuple-element.48, f32[1024]{0:T(1024)S(1)} %copy-done.34), channel_id=3, replica_groups=mesh['stream'=8,'blk'=4] {'stream','blk'}, use_global_device_ids=true, to_apply=%region_13.14.clone | all-reduce | flops 2048 | bytes 16384
  439.6 26.6 %reduce-scatter.13.cloned.1.call-done = f32[32,1024]{1,0:T(8,128)} async-done(((f32[1024,1024]{1,0:T(8,128)}), f32[32,1024]{1,0:T(8,128)}) %reduce-scatter.13.cloned.1.call-update) | async-done | bytes 131088 | tf_op jit(solution)/shard_map/reduce_scatter | solution.py:203
  466.2 149.1 %reduce-scatter.19.cloned.1.call-done = f32[32,1024]{1,0:T(8,128)} async-done(((f32[1024,1024]{1,0:T(8,128)}), f32[32,1024]{1,0:T(8,128)}) %reduce-scatter.19.cloned.1.call-update) | async-done | bytes 131088 | tf_op jit(solution)/shard_map/reduce_scatter | solution.py:206
  615.3 187.2 %reduce-scatter.23.cloned.1.call-done = f32[64,1024]{1,0:T(8,128)} async-done(((f32[2048,1024]{1,0:T(8,128)}), f32[64,1024]{1,0:T(8,128)}) %reduce-scatter.23.cloned.1.call-update) | async-done | bytes 262160 | tf_op jit(solution)/shard_map/reduce_scatter | solution.py:210
  802.5 148.4 %reduce-scatter.15.cloned.1.call-done = f32[32,1024]{1,0:T(8,128)} async-done(((f32[1024,1024]{1,0:T(8,128)}), f32[32,1024]{1,0:T(8,128)}) %reduce-scatter.15.cloned.1.call-update) | async-done | bytes 131088 | tf_op jit(solution)/shard_map/reduce_scatter | solution.py:204
  950.9 149.7 %reduce-scatter.17.cloned.1.call-done = f32[32,1024]{1,0:T(8,128)} async-done(((f32[1024,1024]{1,0:T(8,128)}), f32[32,1024]{1,0:T(8,128)}) %reduce-scatter.17.cloned.1.call-update) | async-done | bytes 131088 | tf_op jit(solution)/shard_map/reduce_scatter | solution.py:205
  1100.6 366.0 %reduce-scatter.21.cloned.1.call-done = f32[32,4096]{1,0:T(8,128)} async-done(((f32[1024,4096]{1,0:T(8,128)}), f32[32,4096]{1,0:T(8,128)}) %reduce-scatter.21.cloned.1.call-update) | async-done | bytes 524304 | tf_op jit(solution)/shard_map/reduce_scatter | solution.py:208
  1466.5 364.9 %reduce-scatter.27.cloned.1.call-done = f32[32,4096]{1,0:T(8,128)} async-done(((f32[1024,4096]{1,0:T(8,128)}), f32[32,4096]{1,0:T(8,128)}) %reduce-scatter.27.cloned.1.call-update) | async-done | bytes 524304
  (152 shorter events, 44.4 us)
Async XLA Ops:
  7.2 72.5 %all-gather.3.cloned.1.call-start = ((), (), s32[]{:S(2)}) async-start(), calls=%async_computation.8 | async-start | bytes 3932160 | tf_op jit(solution)/shard_map/all_gather | solution.py:66
  10.1 6.9 copy-start.30
  10.2 3.2 copy-start.7
  10.2 3.2 copy-start.8
  10.2 3.2 copy-start.13
  10.2 3.2 copy-start.27
  13.3 130.1 %all-gather.5.cloned.1.call-start = ((), (), s32[]{:S(2)}) async-start(), calls=%async_computation.9 | async-start | bytes 3932160 | tf_op jit(solution)/shard_map/all_gather | solution.py:65
  17.0 297.9 %reduce-scatter.25.cloned.1.call-start = ((), (), s32[]{:S(2)}) async-start(), calls=%async_computation.16 | async-start | bytes 7864320
  19.9 128.3 %copy-start.15 = (bf16[128,1024]{0,1:T(8,128)(2,1)}, bf16[128,1024]{0,1:T(8,128)(2,1)S(1)}, u32[]{:S(2)}) copy-start(bf16[128,1024]{0,1:T(8,128)(2,1)S(1)} %copy.64) | copy-start | bytes 786436
  151.6 4.2 copy-start.2
  152.6 6.2 slice-start
  155.7 3.3 slice-start.1
  159.0 13.9 copy-start.28
  161.7 7.7 copy-start.18
  169.4 3.5 copy-start.12
  173.2 5.0 copy-start.36
  178.2 6.0 copy-start.14
  188.0 3.7 copy-start.16
  205.3 260.9 %reduce-scatter.13.cloned.1.call-start = ((), (), s32[]{:S(2)}) async-start(), calls=%async_computation.10 | async-start | bytes 4325376 | tf_op jit(solution)/shard_map/reduce_scatter | solution.py:203
  213.8 401.5 %reduce-scatter.19.cloned.1.call-start = ((), (), s32[]{:S(2)}) async-start(), calls=%async_computation.13 | async-start | bytes 4325376 | tf_op jit(solution)/shard_map/reduce_scatter | solution.py:206
  217.6 585.0 %reduce-scatter.23.cloned.1.call-start = ((), (), s32[]{:S(2)}) async-start(), calls=%async_computation.15 | async-start | bytes 8650752 | tf_op jit(solution)/shard_map/reduce_scatter | solution.py:210
  223.9 104.5 %copy-start.31 = (f32[384]{0:T(512)S(1)}, f32[384]{0:T(512)}, u32[]{:S(2)}) copy-start(f32[384]{0:T(512)} %copy-done.30) | copy-start | bytes 4612
  223.9 727.0 %reduce-scatter.15.cloned.1.call-start = ((), (), s32[]{:S(2)}) async-start(), calls=%async_computation.11 | async-start | bytes 4325376 | tf_op jit(solution)/shard_map/reduce_scatter | solution.py:204
  333.1 767.5 %reduce-scatter.17.cloned.1.call-start = ((), (), s32[]{:S(2)}) async-start(), calls=%async_computation.12 | async-start | bytes 4325376 | tf_op jit(solution)/shard_map/reduce_scatter | solution.py:205
  337.8 1128.8 %reduce-scatter.21.cloned.1.call-start = ((), (), s32[]{:S(2)}) async-start(), calls=%async_computation.14 | async-start | bytes 17301504 | tf_op jit(solution)/shard_map/reduce_scatter | solution.py:208
  347.8 1483.6 %reduce-scatter.27.cloned.1.call-start = ((), (), s32[]{:S(2)}) async-start(), calls=%async_computation.17 | async-start | bytes 17301504
  376.4 4.0 copy-start.6
  376.4 4.0 copy-start.23
  382.0 8.8 copy-start.20
  382.0 8.8 copy-start.38
  393.3 44.3 %copy-start.10 = (f32[1,128,1024]{2,1,0:T(8,128)S(1)}, f32[1,128,1024]{2,1,0:T(8,128)}, u32[]{:S(2)}) copy-start(f32[1,128,1024]{2,1,0:T(8,128)} %copy-done.9) | copy-start | bytes 1572868
  393.3 44.3 %copy-start.37 = (f32[128]{0:T(128)S(1)}, f32[128]{0:T(128)}, u32[]{:S(2)}) copy-start(f32[128]{0:T(128)} %copy-done.36) | copy-start | bytes 1540
  (21 other events, 34.6 us)
Sparse Core Ops, SparseCore 0:
  13.5 66.1 all-gather.2
  81.3 62.1 all-gather.4
  205.4 109.3 reduce-scatter.24
  317.6 148.6 reduce-scatter.12
  468.9 146.3 reduce-scatter.18
  618.0 184.4 reduce-scatter.22
  805.4 145.4 reduce-scatter.14
  953.8 146.7 reduce-scatter.16
  1103.4 363.0 reduce-scatter.20
  1469.2 362.1 reduce-scatter.26
where the time goes:
time: 1850 us; the launch traced here: 1840 us
  waiting for transfers between devices  1600 us (86%)
  matrix products  101 us (5%)
  local copies, waits for them, and re-layouts  63.9 us (3%)
  blocking collectives  41.4 us (2%)
    unnamed x12, waiting for transfers between devices  456 us
    reduce_scatter x1, waiting for transfers between devices, on_device(): lax.psum_scatter(weight_grads[6], ('stream', 'blk'), scatter_dimension=0,...  366 us
    reduce_scatter x1, waiting for transfers between devices, on_device(): lax.psum_scatter(weight_grads[8], ('stream', 'blk'), scatter_dimension=0,...  187 us
    reduce_scatter x1, waiting for transfers between devices, on_device(): lax.psum_scatter(weight_grads[3], ('stream', 'blk'), scatter_dimension=0,...  150 us
    reduce_scatter x1, waiting for transfers between devices, on_device(): lax.psum_scatter(weight_grads[4], ('stream', 'blk'), scatter_dimension=0,...  149 us
    reduce_scatter x1, waiting for transfers between devices, on_device(): lax.psum_scatter(weight_grads[2], ('stream', 'blk'), scatter_dimension=0,...  148 us
    all_gather x1, waiting for transfers between devices, on_device(): lax.all_gather(keys, 'blk', axis=0, tiled=True)  59.3 us
    all_gather x1, waiting for transfers between devices, on_device(): lax.all_gather(values, 'blk', axis=0, tiled=True)  58.7 us
  transfers between devices with their start and end apart: 10, of which 10 were waited for; matrix products, arithmetic and copies ran while one was open for 6% of the time, Pallas kernels for 0%

commit v1 on v0

--- a/solution.py
+++ b/solution.py
@@ -1,14 +1,1239 @@
+import functools
+
 import jax
 import jax.numpy as jnp
 from jax import lax
+from jax.experimental import pallas as pl
+from jax.experimental.pallas import tpu as pltpu
 from jax.sharding import PartitionSpec as P
 
 HD = 128
 RATE = 2
-
+PLANE = 8
 
 epsilon = 1e-05
 masked_score = -1e30
+hidden_slot = 1 << 30
+
+f32 = jnp.float32
+bf16 = jnp.bfloat16
+MIB = 1 << 20
+FLOPS_PER_US = 0.5e9
+VM = pl.BlockSpec(memory_space=pltpu.VMEM)
+SM = pl.BlockSpec(memory_space=pltpu.SMEM)
+ANY = pl.BlockSpec(memory_space=pl.ANY)
+
+
+def dot(left, right, contract=((1,), (0,))):
+    return lax.dot_general(left, right, (contract, ((), ())), preferred_element_type=f32)
+
+
+def standardized(rows):
+    offset = rows - jnp.mean(rows, axis=-1, keepdims=True)
+    scale = lax.rsqrt(jnp.mean(offset * offset, axis=-1, keepdims=True) + epsilon)
+    return offset * scale, scale
+
+
+def norm_input_gradient(e, gain, unit, scale):
+    eg = e * gain
+    return scale * (
+        eg
+        - jnp.mean(eg, axis=-1, keepdims=True)
+        - unit * jnp.mean(eg * unit, axis=-1, keepdims=True)
+    )
+
+
+LOG2E = 1.4426950408889634
+SCORE_SCALE = HD ** (-0.5) * LOG2E
+LAST = ((1,), (1,))
+FIRST = ((0,), (0,))
+TILE = 256
+
+
+def block_of(shape):
+    return pl.BlockSpec(shape, lambda i: (0,) * len(shape))
+
+
+def call(
+    kernel, name, ins, outs, scratch=(), copies=0, grant=24, after=(), cost_us=1.0
+):
+    in_specs, operands = [], []
+    inputs = len(ins)
+
+    def body(*refs):
+        kernel(*refs[:inputs], *refs[inputs + len(after) :])
+
+    for x in ins:
+        far = isinstance(x, tuple)
+        x = x[0] if far else x
+        operands.append(pltpu.with_memory_space_constraint(x, pltpu.HBM) if far else x)
+        in_specs.append(ANY if far else SM if x.size == 1 else block_of(x.shape))
+    operands += after
+    in_specs += [ANY] * len(after)
+    scratch = list(scratch)
+    if copies:
+        scratch.append(pltpu.SemaphoreType.DMA((copies,)))
+    return pl.pallas_call(
+        body,
+        grid=(1,),
+        in_specs=in_specs,
+        out_specs=[ANY if isinstance(o, tuple) else block_of(o.shape) for o in outs],
+        out_shape=[
+            pltpu.HBM(o[0].shape, o[0].dtype) if isinstance(o, tuple) else o for o in outs
+        ],
+        scratch_shapes=scratch,
+        compiler_params=pltpu.CompilerParams(vmem_limit_bytes=grant * MIB),
+        cost_estimate=pl.CostEstimate(
+            flops=int(cost_us * FLOPS_PER_US), bytes_accessed=0, transcendentals=0
+        ),
+        name=name,
+    )(*operands)
+
+
+def gate(arrays, after):
+    count = len(arrays)
+    return pl.pallas_call(
+        lambda *refs: None,
+        in_specs=[ANY] * (count + len(after)),
+        out_specs=[ANY] * count,
+        out_shape=[pltpu.HBM(x.shape, x.dtype) for x in arrays],
+        input_output_aliases={i: i for i in range(count)},
+        compiler_params=pltpu.CompilerParams(vmem_limit_bytes=MIB),
+        cost_estimate=pl.CostEstimate(flops=0, bytes_accessed=0, transcendentals=0),
+        name="gate",
+    )(*arrays, *after)
+
+
+class Copies:
+    def __init__(self, sems):
+        self.sems, self.count = sems, 0
+
+    def __call__(self, source, target):
+        copy = pltpu.make_async_copy(source, target, self.sems.at[self.count])
+        copy.start()
+        self.count += 1
+        return copy
+
+
+def lanes(start, size):
+    return pl.ds(pl.multiple_of(start, size), size)
+
+
+def shape_of(shape, dtype=bf16):
+    return jax.ShapeDtypeStruct(shape, dtype)
+
+
+def norm_rows(raw, gain_ref, normed_ref):
+    rows = raw.shape[1]
+    for i in range(raw.shape[0]):
+        unit, _ = standardized(raw[i].astype(f32))
+        normed_ref[i * rows : (i + 1) * rows, :] = (unit * gain_ref[...]).astype(bf16)
+
+
+ROW_CUTS = 4
+
+
+def bring_rows(bring, source, target):
+    step = source.shape[0] // ROW_CUTS
+    return [
+        bring(source.at[pl.ds(i * step, step)], target.at[pl.ds(i * step, step)])
+        for i in range(ROW_CUTS)
+    ]
+
+
+def wait_all(copies):
+    for copy in copies:
+        copy.wait()
+
+
+def project_kernel(all_queries, *refs):
+    block_ref, *raw_refs = refs[:4]
+    gain_ref, wq_ref, wk_ref, wv_ref = refs[4:8]
+    outs = refs[8:12]
+    wq, wk, wv, normed_ref, q_ref, k_ref, v_ref, raw, sems = refs[12:]
+    bring = Copies(sems)
+    width = k_ref.shape[1]
+    raws = [bring(ref, raw.at[i]) for i, ref in enumerate(raw_refs)]
+    coming = [bring_rows(bring, wk_ref, wk), bring_rows(bring, wv_ref, wv)]
+    if all_queries:
+        query_weight = bring(wq_ref, wq)
+    else:
+        own = q_ref.shape[1]
+        query_weight = bring(wq_ref.at[:, lanes(block_ref[0] * own, own)], wq)
+    wait_all(raws)
+    norm_rows(raw, gain_ref, normed_ref)
+    leaving = [bring(normed_ref, outs[0])]
+    normed = normed_ref[...]
+    for copies, weight, target, out in zip(coming, (wk, wv), (k_ref, v_ref), outs[2:]):
+        wait_all(copies)
+        for at in range(0, width, TILE):
+            target[:, at : at + TILE] = dot(normed, weight[:, at : at + TILE]).astype(bf16)
+        leaving.append(bring(target, out))
+    query_weight.wait()
+    q_ref[...] = dot(normed[2 * raw.shape[1] :], wq[...]).astype(bf16)
+    leaving.append(bring(q_ref, outs[1]))
+    wait_all(leaving)
+
+
+def projected_shapes(rows, width, own):
+    return [
+        shape_of((3 * rows, width)),
+        shape_of((rows, own)),
+        shape_of((3 * rows, width)),
+        shape_of((3 * rows, width)),
+    ]
+
+
+def project(block, raw_rows, gain, w_query, w_key, w_value, own, after):
+    rows, width = raw_rows[0].shape
+    shapes = projected_shapes(rows, width, own)
+    weights = [(width, own), (width, width), (width, width)]
+    return call(
+        functools.partial(project_kernel, own == width),
+        "project",
+        [block] + [(x,) for x in raw_rows] + [gain, (w_query,), (w_key,), (w_value,)],
+        [(x,) for x in shapes],
+        scratch=[pltpu.VMEM(x, bf16) for x in weights]
+        + [pltpu.VMEM(x.shape, x.dtype) for x in shapes]
+        + [pltpu.VMEM((3, rows, width), bf16)],
+        copies=2 * ROW_CUTS + 8,
+        after=after,
+        cost_us=0.1,
+    )
+
+
+def compress_kernel(pairs_ref, w_far, out_ref, w_ref, sems):
+    bring = Copies(sems)
+    count = w_ref.shape[0]
+    coming = [bring(w_far.at[pl.ds(i * w_ref.shape[1], w_ref.shape[1])], w_ref.at[i]) for i in range(count)]
+    total = None
+    for i in range(count):
+        coming[i].wait()
+        part = dot(pairs_ref[:, i * w_ref.shape[1] : (i + 1) * w_ref.shape[1]], w_ref[i])
+        total = part if total is None else total + part
+    out_ref[...] = total.astype(bf16)
+
+
+def compress(pairs, w_compress, after):
+    depth, width = w_compress.shape
+    count = 4
+    return call(
+        compress_kernel,
+        "compress",
+        [pairs, (w_compress,)],
+        [shape_of((pairs.shape[0], width))],
+        scratch=[pltpu.VMEM((count, depth // count, width), bf16)],
+        copies=count,
+        after=after,
+        cost_us=3.2,
+    )[0]
+
+
+def score_bias(qdoc, qpos, kdoc_ref, kpos_ref, slot):
+    allowed = (kdoc_ref[slot : slot + 1, :] == qdoc) & (kpos_ref[slot : slot + 1, :] <= qpos)
+    return jnp.where(allowed, 0.0, masked_score)
+
+
+def attend_kernel(slots, *refs):
+    qdoc_ref, qpos_ref, kdoc_ref, kpos_ref, q_far = refs[:5]
+    k_far = refs[5 : 5 + slots]
+    v_far = refs[5 + slots : 5 + 2 * slots]
+    out_ref, stat_ref, bias_ref, q_ref, k_ref, v_ref, sems = refs[5 + 2 * slots :]
+    rows, width = q_ref.shape
+    bring = Copies(sems)
+    query = bring(q_far, q_ref)
+    tiles = [slice(at, at + TILE) for at in range(0, width, TILE)]
+    coming = [
+        [
+            bring(far[slot].at[:, at], near.at[slot, :, at])
+            for slot in range(slots)
+            for far, near in ((k_far, k_ref), (v_far, v_ref))
+        ]
+        for at in tiles
+    ]
+    qdoc, qpos = qdoc_ref[:rows, :], qpos_ref[:rows, :]
+    for slot in range(slots):
+        bias_ref[slot] = score_bias(qdoc, qpos, kdoc_ref, kpos_ref, slot)
+    query.wait()
+    lane = lax.broadcasted_iota(jnp.int32, (rows, HD), 1)
+    stats = jnp.zeros((rows, HD), f32)
+    heads = width // HD
+    for head in range(heads):
+        if head * HD % TILE == 0:
+            for copy in coming[head * HD // TILE]:
+                copy.wait()
+        at = slice(head * HD, (head + 1) * HD)
+        q = q_ref[:, at]
+        scores = [
+            dot(q, k_ref[slot, :, at], LAST) * SCORE_SCALE + bias_ref[slot]
+            for slot in range(slots)
+        ]
+        top = functools.reduce(jnp.maximum, scores)
+        top = jnp.max(top, axis=-1, keepdims=True)
+        weights = [jnp.exp2(s - top) for s in scores]
+        total = jnp.sum(functools.reduce(jnp.add, weights), axis=-1, keepdims=True)
+        out_ref[:, at] = functools.reduce(
+            jnp.add,
+            [dot(weights[slot].astype(bf16), v_ref[slot, :, at]) for slot in range(slots)],
+        )
+        stats = jnp.where(lane == head, top, stats)
+        stats = jnp.where(lane == heads + head, total, stats)
+    stat_ref[...] = stats
+
+
+def attend(query, keys, values, marks, after):
+    slots = len(keys)
+    rows, width = query.shape
+    key_rows = keys[0].shape[0]
+    return call(
+        functools.partial(attend_kernel, slots),
+        "attend",
+        [*marks, (query,)] + [(x,) for x in (*keys, *values)],
+        [shape_of((rows, width), f32), shape_of((rows, HD), f32)],
+        scratch=[
+            pltpu.VMEM((slots, rows, key_rows), f32),
+            pltpu.VMEM((rows, width), bf16),
+            pltpu.VMEM((slots, key_rows, width), bf16),
+            pltpu.VMEM((slots, key_rows, width), bf16),
+        ],
+        copies=1 + 2 * slots * (width // TILE),
+        after=after,
+        cost_us=0.1,
+    )
+
+
+def finish_kernel(slot, *refs):
+    block_ref, *raw_refs = refs[:4]
+    gain_ref, wq_far, wk_far, wv_far = refs[4:8]
+    query_far, sum_ref, stat_ref, qdoc_ref, qpos_ref, kdoc_ref, kpos_ref = refs[8:15]
+    seg_ref, wo_far, gain_ffn_ref = refs[15:18]
+    outs = refs[18:23]
+    middle_ref, nf_ref = refs[23:25]
+    wq, wk, wv, normed_ref, q_ref, k_ref, v_ref, wo, query_ref, att_ref, raw, sems = refs[25:]
+    rows, width = query_ref.shape
+    bring = Copies(sems)
+    raws = [bring(ref, raw.at[i]) for i, ref in enumerate(raw_refs)]
+    coming = [bring_rows(bring, wk_far, wk), bring_rows(bring, wv_far, wv)]
+    query = bring(query_far, query_ref)
+    output_weight = bring(wo_far, wo)
+    own = q_ref.shape[1]
+    query_weight = bring(wq_far.at[:, lanes(block_ref[0] * own, own)], wq)
+    bias = score_bias(qdoc_ref[:rows, :], qpos_ref[:rows, :], kdoc_ref, kpos_ref, slot)
+    wait_all(raws)
+    norm_rows(raw, gain_ref, normed_ref)
+    leaving = [bring(normed_ref, outs[0])]
+    normed = normed_ref[...]
+    query.wait()
+    heads = width // HD
+    for copies, weight, target, out in zip(coming, (wk, wv), (k_ref, v_ref), outs[2:4]):
+        wait_all(copies)
+        for at in range(0, width, TILE):
+            target[:, at : at + TILE] = dot(normed, weight[:, at : at + TILE]).astype(bf16)
+        leaving.append(bring(target, out))
+    group = 4
+    for start in range(0, heads, group):
+        some = range(start, start + group)
+        at = {h: slice(h * HD, (h + 1) * HD) for h in some}
+        scores = {
+            h: dot(query_ref[:, at[h]], k_ref[:, at[h]], LAST) * SCORE_SCALE + bias for h in some
+        }
+        before = {h: stat_ref[:, h : h + 1] for h in some}
+        top = {
+            h: jnp.maximum(before[h], jnp.max(scores[h], axis=-1, keepdims=True)) for h in some
+        }
+        weights = {h: jnp.exp2(scores[h] - top[h]) for h in some}
+        shrink = {h: jnp.exp2(before[h] - top[h]) for h in some}
+        total = {
+            h: stat_ref[:, heads + h : heads + h + 1] * shrink[h]
+            + jnp.sum(weights[h], axis=-1, keepdims=True)
+            for h in some
+        }
+        out = {
+            h: sum_ref[:, at[h]] * shrink[h] + dot(weights[h].astype(bf16), v_ref[:, at[h]])
+            for h in some
+        }
+        for h in some:
+            att_ref[:, at[h]] = (out[h] * (1.0 / total[h])).astype(bf16)
+    query_weight.wait()
+    q_ref[...] = dot(normed[2 * raw.shape[1] :], wq[...]).astype(bf16)
+    leaving.append(bring(q_ref, outs[1]))
+    leaving.append(bring(att_ref, outs[4]))
+    output_weight.wait()
+    middle = seg_ref[...].astype(f32) + dot(att_ref[...], wo[...])
+    middle_ref[...] = middle
+    unit, _ = standardized(middle)
+    nf_ref[...] = (unit * gain_ffn_ref[...]).astype(bf16)
+    wait_all(leaving)
+
+
+def finish(
+    slot, block, raw_rows, gain, w_query, w_key, w_value, own, query, partial, marks, segment, w_output, gain_ffn, after
+):
+    rows, width = segment.shape
+    shapes = projected_shapes(rows, width, own)
+    weights = [(width, own), (width, width), (width, width)]
+    return call(
+        functools.partial(finish_kernel, slot),
+        "finish",
+        [block] + [(x,) for x in raw_rows] + [gain, (w_query,), (w_key,), (w_value,), (query,), *partial, *marks]
+        + [segment, (w_output,), gain_ffn],
+        [(x,) for x in shapes]
+        + [(shape_of((rows, width)),), shape_of((rows, width), f32), shape_of((rows, width))],
+        scratch=[pltpu.VMEM(x, bf16) for x in weights]
+        + [pltpu.VMEM(x.shape, x.dtype) for x in shapes]
+        + [
+            pltpu.VMEM((width, width), bf16),
+            pltpu.VMEM((rows, width), bf16),
+            pltpu.VMEM((rows, width), bf16),
+            pltpu.VMEM((3, rows, width), bf16),
+        ],
+        copies=2 * ROW_CUTS + 11,
+        after=after,
+        cost_us=9.0,
+    )
+
+
+def feed_kernel(chips, place_ref, nf_own, nf_got, cot_own, cot_got, we_far, wr_far, *refs):
+    both_far = refs[:chips]
+    res_ref, dn_ref, send_ref, nf_ref, cot_ref, both, we, wr, sems = refs[chips:]
+    rows = nf_own.shape[0]
+    tile = wr.shape[1]
+    bring = Copies(sems)
+    coming = []
+
+    def ahead(chip):
+        if chip < chips:
+            at = lanes((place_ref[0] ^ (2 * chip)) * tile, tile)
+            coming.append(
+                (
+                    bring(we_far.at[:, at], we.at[chip]),
+                    bring(wr_far.at[at, :], wr.at[chip]),
+                )
+            )
+
+    ahead(0)
+    ahead(1)
+    nf_ref[:rows] = nf_own[...]
+    nf_ref[rows:] = nf_got[...]
+    cot_ref[:rows] = cot_own[...]
+    cot_ref[rows:] = cot_got[...]
+    part = tile // 2
+    leaving = []
+    res = dn = None
+    for chip in range(chips):
+        wait_all(coming[chip])
+        ahead(chip + 2)
+        for at in range(0, tile, part):
+            here = slice(at, at + part)
+            hidden = dot(nf_ref[...], we[chip, :, here])
+            d_act = dot(cot_ref[...], wr[chip, here, :], LAST)
+            cdf = 0.5 + 0.5 * lax.erf(hidden * (0.5**0.5))
+            density = jnp.exp2(hidden * hidden * (-0.5 * LOG2E)) * 0.3989422804014327
+            both[chip, 0, :, here] = (hidden * cdf).astype(bf16)
+            both[chip, 1, :, here] = (
+                d_act * (cdf + hidden * density)
+            ).astype(bf16)
+        leaving.append(bring(both.at[chip], both_far[chip]))
+        res_part = dot(both[chip, 0], wr[chip])
+        dn_part = dot(both[chip, 1], we[chip], LAST)
+        res = res_part if chip == 0 else res + res_part
+        dn = dn_part if chip == 0 else dn + dn_part
+    res_ref[...] = res[:rows]
+    dn_ref[...] = dn[:rows]
+    send_ref[0] = res[rows:].astype(bf16)
+    send_ref[1] = dn[rows:].astype(bf16)
+    wait_all(leaving)
+
+
+def feed(place, nf_own, nf_got, cot_own, cot_got, w_expand, w_reduce, after):
+    rows, width = nf_own.shape
+    chips = PLANE // 2
+    tile = w_expand.shape[1] // PLANE
+    return call(
+        functools.partial(feed_kernel, chips),
+        "feed",
+        [place, nf_own, nf_got, cot_own, cot_got, (w_expand,), (w_reduce,)],
+        [(shape_of((2, 2 * rows, tile)),)] * chips
+        + [shape_of((rows, width), f32)] * 2
+        + [shape_of((2, rows, width))],
+        scratch=[
+            pltpu.VMEM((2 * rows, width), bf16),
+            pltpu.VMEM((2 * rows, width), bf16),
+            pltpu.VMEM((chips, 2, 2 * rows, tile), bf16),
+            pltpu.VMEM((chips, width, tile), bf16),
+            pltpu.VMEM((chips, tile, width), bf16),
+        ],
+        copies=3 * chips,
+        grant=28,
+        after=after,
+        cost_us=8.0,
+    )
+
+
+def leave_kernel(slots, block_ref, *refs):
+    res_ref, dn_ref, got_ref, middle_ref, cot_ref, gain_ref, wo_far = refs[:7]
+    result_ref, dmid_far, branch_far = refs[7:10]
+    datt_refs = refs[10 : 10 + slots]
+    wo, dmid_ref, branch_ref, sems = refs[10 + slots :]
+    own = wo.shape[1]
+    bring = Copies(sems)
+    coming = [
+        bring(wo_far.at[lanes(lax.rem(block_ref[0] + slot, slots) * own, own), :], wo.at[slot])
+        for slot in range(slots)
+    ]
+    middle = middle_ref[...]
+    result_ref[...] = (middle + (res_ref[...] + got_ref[0].astype(f32))).astype(bf16)
+    unit, scale = standardized(middle)
+    d_normed = dn_ref[...] + got_ref[1].astype(f32)
+    d_mid = cot_ref[...].astype(f32) + norm_input_gradient(d_normed, gain_ref[...], unit, scale)
+    dmid_ref[...] = d_mid
+    branch = d_mid.astype(bf16)
+    branch_ref[...] = branch
+    leaving = [bring(dmid_ref, dmid_far), bring(branch_ref, branch_far)]
+    for slot in range(slots):
+        coming[slot].wait()
+        datt_refs[slot][...] = dot(branch, wo[slot], LAST).astype(bf16)
+    wait_all(leaving)
+
+
+def leave(block, slots, res, dn, got, middle, cotangent, gain, w_output, after):
+    rows, width = middle.shape
+    own = width // slots
+    return call(
+        functools.partial(leave_kernel, slots),
+        "leave",
+        [block, res, dn, got, middle, cotangent, gain, (w_output,)],
+        [shape_of((rows, width)), (shape_of((rows, width), f32),), (shape_of((rows, width)),)]
+        + [shape_of((rows, own))] * slots,
+        scratch=[
+            pltpu.VMEM((slots, own, width), bf16),
+            pltpu.VMEM((rows, width), f32),
+            pltpu.VMEM((rows, width), bf16),
+        ],
+        copies=slots + 2,
+        after=after,
+        cost_us=3.8,
+    )
+
+
+def attend_back_kernel(slots, heads, block_ref, *refs):
+    take = iter(refs)
+    marks = [next(take) for _ in range(4)]
+    g_refs = [next(take) for _ in range(slots)]
+    q_far = [next(take) for _ in range(slots)]
+    k_far = [next(take) for _ in range(slots)]
+    v_far = [next(take) for _ in range(slots)]
+    piece_far = [next(take) for _ in range(slots)]
+    dk_far, dv_far, q_ref, k_ref, v_ref, piece_refs, dk_ref, dv_ref, sems = take
+    qdoc_ref, qpos_ref, kdoc_ref, kpos_ref = marks
+    scale = HD ** (-0.5)
+    rows = g_refs[0].shape[0]
+    own = heads * HD
+    bring = Copies(sems)
+    owned = lanes(block_ref[0] * own, own)
+    coming = []
+    for slot in range(slots):
+        coming.append(bring(q_far[slot].at[:, owned] if slot == 0 else q_far[slot], q_ref.at[slot]))
+        coming.append(bring(k_far[slot].at[:, owned], k_ref.at[slot]))
+        coming.append(bring(v_far[slot].at[:, owned], v_ref.at[slot]))
+    for copy in coming:
+        copy.wait()
+    dk = [[None] * slots for _ in range(heads)]
+    dv = [[None] * slots for _ in range(heads)]
+    for one in range(slots):
+        here = slice(one * rows, (one + 1) * rows)
+        qdoc, qpos = qdoc_ref[here, :], qpos_ref[here, :]
+        bias = [score_bias(qdoc, qpos, kdoc_ref, kpos_ref, slot) for slot in range(slots)]
+        for head in range(heads):
+            at = slice(head * HD, (head + 1) * HD)
+            q = q_ref[one, :, at]
+            grad = g_refs[one][:, at]
+            scores = [
+                dot(q, k_ref[slot, :, at], LAST) * SCORE_SCALE + bias[slot]
+                for slot in range(slots)
+            ]
+            top = jnp.max(functools.reduce(jnp.maximum, scores), axis=-1, keepdims=True)
+            weights = [jnp.exp2(s - top) for s in scores]
+            total = jnp.sum(functools.reduce(jnp.add, weights), axis=-1, keepdims=True)
+            inverse = 1.0 / total
+            probs = [w * inverse for w in weights]
+            d_probs = [dot(grad, v_ref[slot, :, at], LAST) for slot in range(slots)]
+            delta = jnp.sum(
+                functools.reduce(jnp.add, [p * d for p, d in zip(probs, d_probs)]),
+                axis=-1,
+                keepdims=True,
+            )
+            dq = None
+            for slot in range(slots):
+                d_score = (probs[slot] * (d_probs[slot] - delta)).astype(bf16)
+                part = dot(d_score, k_ref[slot, :, at])
+                dq = part if dq is None else dq + part
+                dk_part = dot(d_score, q, FIRST)
+                dv_part = dot(probs[slot].astype(bf16), grad, FIRST)
+                dk[head][slot] = dk_part if one == 0 else dk[head][slot] + dk_part
+                dv[head][slot] = dv_part if one == 0 else dv[head][slot] + dv_part
+            piece_refs[one, :, at] = (dq * scale).astype(bf16)
+    leaving = []
+    for slot in range(slots):
+        for head in range(heads):
+            at = slice(head * HD, (head + 1) * HD)
+            d_key = (dk[head][slot] * scale).astype(bf16)
+            d_value = dv[head][slot].astype(bf16)
+            dk_ref[slot, :, at] = d_key
+            dv_ref[slot, :, at] = d_value
+            for i, value in enumerate((d_key, d_value)):
+                first = (i + 1) * own + head * HD
+                piece_refs[slot, :, first : first + HD] = value[2 * rows :]
+        leaving.append(bring(piece_refs.at[slot], piece_far[slot]))
+    leaving += [bring(dk_ref, dk_far), bring(dv_ref, dv_far)]
+    wait_all(leaving)
+
+
+def attend_back(block, queries, grads, keys, values, marks, after):
+    slots = len(keys)
+    key_rows = keys[0].shape[0]
+    rows, own = grads[0].shape
+    heads = own // HD
+    return call(
+        functools.partial(attend_back_kernel, slots, heads),
+        "attend_back",
+        [block, *marks, *grads] + [(x,) for x in (*queries, *keys, *values)],
+        [(shape_of((rows, 3 * own)),)] * slots + [(shape_of((slots, key_rows, own)),)] * 2,
+        scratch=[
+            pltpu.VMEM((slots, rows, own), bf16),
+            pltpu.VMEM((slots, key_rows, own), bf16),
+            pltpu.VMEM((slots, key_rows, own), bf16),
+            pltpu.VMEM((slots, rows, 3 * own), bf16),
+            pltpu.VMEM((slots, key_rows, own), bf16),
+            pltpu.VMEM((slots, key_rows, own), bf16),
+        ],
+        copies=4 * slots + 2,
+        after=after,
+        cost_us=4.0,
+    )
+
+
+def heads_kernel(slots, place_ref, *refs):
+    piece_far = refs[:slots]
+    normed_far = refs[slots : 2 * slots]
+    dk_far, dv_far = refs[2 * slots : 2 * slots + 2]
+    keep_far, give_far, out_ref, pieces, normed, dk, dv, sems = refs[2 * slots + 2 :]
+    own = dk.shape[2]
+    rows = pieces.shape[1]
+    cut = out_ref.shape[2]
+    core = lax.rem(place_ref[0], 2)
+    bring = Copies(sems)
+    second = [bring(normed_far[0], normed.at[0]), bring(dv_far, dv)]
+    second += [bring(normed_far[slot], normed.at[slot]) for slot in range(1, slots)]
+    third = [bring(dk_far, dk)]
+    fourth = [bring(piece_far[slot], pieces.at[slot]) for slot in range(slots)]
+    leaving = []
+
+    def store(value, at):
+        value = value.astype(bf16)
+        here = slice(at, at + value.shape[1])
+        for j in range(value.shape[0] // cut):
+            out_ref[j % 2, j // 2, :, here] = value[j * cut : (j + 1) * cut]
+        here = pl.ds(at, value.shape[1])
+        leaving.append(bring(out_ref.at[1 - core, :, :, here], give_far.at[:, :, here]))
+        leaving.append(bring(out_ref.at[core, :, :, here], keep_far.at[:, :, here]))
+
+    def over_slots(part):
+        total = part(0)
+        for slot in range(1, slots):
+            total = total + part(slot)
+        return total
+
+    wait_all(second)
+    store(over_slots(lambda slot: dot(normed[slot], dv[slot], FIRST)), 2 * own)
+    wait_all(third)
+    store(over_slots(lambda slot: dot(normed[slot], dk[slot], FIRST)), own)
+    wait_all(fourth)
+    store(over_slots(lambda slot: dot(normed[slot, 2 * rows :], pieces[slot, :, :own], FIRST)), 0)
+    wait_all(leaving)
+
+
+def heads_gradient(place, normed, pieces, dk, dv, cut, after):
+    slots, key_rows, own = dk.shape
+    rows = pieces[0].shape[0]
+    width = normed[0].shape[1]
+    half = (width // cut // 2, cut, 3 * own)
+    return call(
+        functools.partial(heads_kernel, slots),
+        "heads_gradient",
+        [place] + [(x,) for x in (*pieces, *normed, dk, dv)],
+        [(shape_of(half),)] * 2,
+        scratch=[
+            pltpu.VMEM((2, *half), bf16),
+            pltpu.VMEM((slots, rows, 3 * own), bf16),
+            pltpu.VMEM((slots, key_rows, width), bf16),
+            pltpu.VMEM((slots, key_rows, own), bf16),
+            pltpu.VMEM((slots, key_rows, own), bf16),
+        ],
+        copies=2 * slots + 8,
+        after=after,
+        grant=36,
+        cost_us=0.1,
+    )
+
+
+def output_kernel(place_ref, att_far, branch_far, keep_far, give_far, out_ref, att, branch, sems):
+    core = lax.rem(place_ref[0], 2)
+    cut = out_ref.shape[2]
+    bring = Copies(sems)
+    wait_all([bring(att_far, att), bring(branch_far, branch)])
+    step = 2 * cut
+    leaving = []
+    for i in range(out_ref.shape[1]):
+        at = slice(i * step, (i + 1) * step)
+        value = dot(att[:, at], branch[...], FIRST).astype(bf16)
+        for j in range(2):
+            out_ref[j, i] = value[j * cut : (j + 1) * cut]
+        leaving.append(bring(out_ref.at[1 - core, i], give_far.at[i]))
+        leaving.append(bring(out_ref.at[core, i], keep_far.at[i]))
+    wait_all(leaving)
+
+
+def output_gradient(place, attended, branch, cut, after):
+    rows, width = attended.shape
+    half = (width // cut // 2, cut, width)
+    return call(
+        output_kernel,
+        "output_gradient",
+        [place, (attended,), (branch,)],
+        [(shape_of(half),)] * 2,
+        scratch=[
+            pltpu.VMEM((2, *half), bf16),
+            pltpu.VMEM((rows, width), bf16),
+            pltpu.VMEM((rows, width), bf16),
+        ],
+        copies=2 + 2 * half[0],
+        after=after,
+        cost_us=2.8,
+    )
+
+
+def pair_add_kernel(place_ref, *refs):
+    keep_far = refs[:2]
+    got = refs[2:4]
+    outs = refs[4:8]
+    near = refs[8:10]
+    total, sems = refs[10:]
+    bring = Copies(sems)
+    chip = place_ref[0] // 2
+    order = [1, 2, 3, 0]
+    coming = {j: [bring(f.at[chip ^ j], n.at[j]) for f, n in zip(keep_far, near)] for j in order}
+    leaving = []
+    width = near[0].shape[2]
+    for j in order:
+        wait_all(coming[j])
+        for at, a, b in zip((slice(0, width), slice(width, None)), near, got):
+            total[j, :, at] = (a[j].astype(f32) + b[chip ^ j].astype(f32)).astype(bf16)
+        leaving.append(bring(total.at[j], outs[j]))
+    wait_all(leaving)
+
+
+def pair_add(place, qkv_keep, qkv_got, output_keep, output_got, after):
+    chips, rows, width = qkv_keep.shape
+    wide = output_keep.shape[2]
+    return call(
+        pair_add_kernel,
+        "pair_add",
+        [place, (qkv_keep,), (output_keep,), qkv_got, output_got],
+        [(shape_of((rows, width + wide)),)] * chips,
+        scratch=[
+            pltpu.VMEM(qkv_keep.shape, bf16),
+            pltpu.VMEM(output_keep.shape, bf16),
+            pltpu.VMEM((chips, rows, width + wide), bf16),
+        ],
+        copies=3 * chips,
+        after=after,
+        cost_us=3.0,
+    )
+
+
+def chip_add_kernel(chips, block_ref, *refs):
+    pieces = refs[:chips]
+    outs = refs[chips:-1]
+    total = refs[-1]
+    total[...] = sum(p[...].astype(f32) for p in pieces)
+    blocks = len(outs)
+    rows = total.shape[0] // blocks
+    for k in range(blocks):
+        outs[k][...] = total[lanes((block_ref[0] ^ k) * rows, rows), :].astype(bf16)
+
+
+def chip_add(block, blocks, pieces, after):
+    rows, width = pieces[0].shape
+    return call(
+        functools.partial(chip_add_kernel, len(pieces)),
+        "chip_add",
+        [block, *pieces],
+        [shape_of((rows // blocks, width))] * blocks,
+        scratch=[pltpu.VMEM((rows, width), f32)],
+        after=after,
+        cost_us=0.1,
+    )
+
+
+def last_heads_kernel(blocks, block_ref, *refs):
+    parts = refs[:blocks]
+    gain_ref = refs[blocks]
+    weights_far = refs[blocks + 1 : blocks + 4]
+    at_ref = refs[blocks + 4]
+    outs = refs[blocks + 5 : blocks + 8]
+    output_ref, norm_ref, weights, sems = refs[blocks + 8 :]
+    rows, width = output_ref.shape
+    own = width // blocks
+    bring = Copies(sems)
+    here = pl.ds(pl.multiple_of(at_ref[0] * rows, rows), rows)
+    coming = [bring(far.at[here, :], weights.at[i]) for i, far in enumerate(weights_far)]
+    for k in range(blocks):
+        at = lanes((block_ref[0] ^ k) * own, own)
+        for i in range(3):
+            outs[i][:, at] = parts[k][:, i * own : (i + 1) * own].astype(f32)
+    first = 3 * own
+    output_ref[...] = sum(p[:, first : first + width].astype(f32) for p in parts)
+    wait_all(coming)
+    total = sum(weights[i].astype(f32) * outs[i][...] for i in range(3))
+    norm_ref[...] = jnp.sum(total, axis=1, keepdims=True) / gain_ref[...]
+
+
+def last_heads(block, index, parts, gain, w_query, w_key, w_value, after):
+    blocks = len(parts)
+    rows = parts[0].shape[0]
+    width = w_query.shape[0]
+    return call(
+        functools.partial(last_heads_kernel, blocks),
+        "last_heads",
+        [block, *parts, gain, (w_query,), (w_key,), (w_value,), index],
+        [shape_of((rows, width), f32)] * 4 + [shape_of((rows, 1), f32)],
+        scratch=[pltpu.VMEM((3, rows, width), bf16)],
+        copies=3,
+        after=after,
+        cost_us=1.8,
+    )
+
+
+def segment_kernel(slots, block_ref, *refs):
+    pieces_far = refs[:slots]
+    seg_ref, gain_ref, dmid_far = refs[slots : slots + 3]
+    far = refs[slots + 3 : slots + 6]
+    out_ref, weight, pieces, dmid_ref, sems = refs[slots + 6 :]
+    own = pieces.shape[2] // 3
+    bring = Copies(sems)
+    coming = []
+    for slot in range(slots):
+        at = lanes(lax.rem(block_ref[0] + slot, slots) * own, own)
+        bring_piece = bring(pieces_far[slot], pieces.at[slot])
+        coming.append([bring(far[i].at[:, at], weight.at[slot, i]) for i in range(3)])
+        coming[-1].append(bring_piece)
+    middle = bring(dmid_far, dmid_ref)
+    total = None
+    for slot in range(slots):
+        wait_all(coming[slot])
+        for i in range(3):
+            part = dot(pieces[slot, :, i * own : (i + 1) * own], weight[slot, i], LAST)
+            total = part if total is None else total + part
+    unit, scale = standardized(seg_ref[...].astype(f32))
+    middle.wait()
+    out_ref[...] = (
+        dmid_ref[...] + norm_input_gradient(total, gain_ref[...], unit, scale)
+    ).astype(bf16)
+
+
+def segment_gradient(block, pieces, w_query, w_key, w_value, segment, gain, d_middle, after):
+    slots = len(pieces)
+    rows, width = segment.shape
+    return call(
+        functools.partial(segment_kernel, slots),
+        "segment_gradient",
+        [block]
+        + [(x,) for x in pieces]
+        + [segment, gain, (d_middle,), (w_query,), (w_key,), (w_value,)],
+        [shape_of((rows, width))],
+        scratch=[
+            pltpu.VMEM((slots, 3, width, width // slots), bf16),
+            pltpu.VMEM((slots, *pieces[0].shape), bf16),
+            pltpu.VMEM((rows, width), f32),
+        ],
+        copies=4 * slots + 1,
+        after=after,
+        cost_us=4.8,
+    )[0]
+
+
+def plane_kernel(blocks, block_ref, *refs):
+    chips = PLANE // 2
+    left_far = refs[: 2 * PLANE]
+    right_far = refs[2 * PLANE : 2 * PLANE + chips]
+    out_far, first_r, first_e, out_ref, left, right, sems = refs[2 * PLANE + chips :]
+    rows = left_far[0].shape[0]
+    bring = Copies(sems)
+    coming = [[], []]
+    for i in range(2):
+        for chip in range(chips):
+            at = pl.ds(2 * chip * rows, 2 * rows)
+            coming[i].append(bring(right_far[chip].at[i], right.at[i, at]))
+        for j in range(PLANE):
+            at = pl.ds(j * rows, rows)
+            coming[i].append(bring(left_far[i * PLANE + j], left.at[i, at]))
+    cut = out_ref.shape[3]
+    width = left.shape[2]
+    step = width // 4
+    leaving = []
+    for i in range(2):
+        wait_all(coming[i])
+        for at in range(0, width, step):
+            value = dot(left[i, :, at : at + step], right[i], FIRST).astype(bf16)
+            for part in range(step // cut):
+                j = at // cut + part
+                out_ref[j % blocks, i, j // blocks] = value[part * cut : (part + 1) * cut]
+    leaving.append(bring(out_ref, out_far))
+    start = lax.rem(block_ref[0] + blocks - 1, blocks)
+    first_r[...] = out_ref[start, 0]
+    first_e[...] = out_ref[start, 1]
+    wait_all(leaving)
+
+
+def plane_gradients(block, cots, nfs, both, blocks, cut, after):
+    rows, width = cots[0].shape
+    _, _, tile = both[0].shape
+    out = (blocks, 2, width // (blocks * cut), cut, tile)
+    return call(
+        functools.partial(plane_kernel, blocks),
+        "plane_gradients",
+        [block] + [(x,) for x in (*cots, *nfs, *both)],
+        [(shape_of(out),), shape_of(out[2:]), shape_of(out[2:])],
+        scratch=[
+            pltpu.VMEM(out, bf16),
+            pltpu.VMEM((2, PLANE * rows, width), bf16),
+            pltpu.VMEM((2, PLANE * rows, tile), bf16),
+        ],
+        copies=2 * PLANE + PLANE + 1,
+        after=after,
+        cost_us=0.1,
+    )
+
+
+def ring_kernel(which, k, blocks, block_ref, moved_ref, part_far, out_ref, part_ref, sems):
+    bring = Copies(sems)
+    piece = lax.rem(block_ref[0] + 2 * blocks - k, blocks)
+    bring(part_far.at[piece, which], part_ref).wait()
+    out_ref[...] = (moved_ref[...].astype(f32) + part_ref[...].astype(f32)).astype(bf16)
+
+
+def ring_add(block, which, k, moved, part, after):
+    blocks = part.shape[0]
+    return call(
+        functools.partial(ring_kernel, which, k, blocks),
+        "ring_add",
+        [block, moved, (part,)],
+        [shape_of(moved.shape)],
+        scratch=[pltpu.VMEM(moved.shape, bf16)],
+        copies=1,
+        after=after,
+    )[0]
+
+
+def compress_gradient_kernel(place_ref, pairs_own, pairs_got, comp_own, comp_got, *refs):
+    outs = refs[:-2]
+    left, right = refs[-2:]
+    rows = pairs_own.shape[0]
+    cut = left.shape[2]
+    right[:rows] = comp_own[...]
+    right[rows:] = comp_got[...]
+    for chip in range(len(outs)):
+        at = lanes((place_ref[0] ^ (2 * chip)) * cut, cut)
+        left[chip, :rows] = pairs_own[:, at]
+        left[chip, rows:] = pairs_got[:, at]
+        outs[chip][...] = dot(left[chip], right[...], FIRST).astype(bf16)
+
+
+def compress_gradient(place, pairs_own, pairs_got, comp_own, comp_got, after):
+    rows, depth = pairs_own.shape
+    width = comp_own.shape[1]
+    chips = PLANE // 2
+    cut = depth // PLANE
+    return call(
+        compress_gradient_kernel,
+        "compress_gradient",
+        [place, pairs_own, pairs_got, comp_own, comp_got],
+        [shape_of((cut, width))] * chips,
+        scratch=[pltpu.VMEM((chips, 2 * rows, cut), bf16), pltpu.VMEM((2 * rows, width), bf16)],
+        after=after,
+        cost_us=1.5,
+    )
+
+
+def spread_kernel(place_ref, block_ref, r_moved, e_moved, part_far, *refs):
+    outs = refs[:PLANE]
+    part_ref, sems = refs[PLANE:]
+    bring = Copies(sems)
+    bring(part_far.at[block_ref[0]], part_ref).wait()
+    for j in range(PLANE):
+        at = place_ref[0] ^ j
+        for i, moved in enumerate((r_moved, e_moved)):
+            outs[j][i] = (part_ref[i, at].astype(f32) + moved[at].astype(f32)).astype(bf16)
+
+
+def spread(place, block, moved, part, after):
+    count, rows, tile = moved[0].shape
+    return call(
+        spread_kernel,
+        "spread",
+        [place, block, *moved, (part,)],
+        [shape_of((2, rows, tile))] * count,
+        scratch=[pltpu.VMEM((2, count, rows, tile), bf16)],
+        copies=1,
+        after=after,
+        cost_us=1.2,
+    )
+
+
+def last_wide_kernel(place_ref, index_ref, *refs):
+    parts = refs[:PLANE]
+    gain_ref, weight_far, expand_ref, reduce_ref, gain_out, weight, sems = refs[PLANE:]
+    rows = weight.shape[0]
+    tile = parts[0].shape[2]
+    bring = Copies(sems)
+    coming = bring(
+        weight_far.at[pl.ds(pl.multiple_of(index_ref[0] * rows, rows), rows), :], weight
+    )
+    for j in range(PLANE):
+        at = lanes((place_ref[0] ^ j) * tile, tile)
+        reduce_ref[:, at] = parts[j][0].astype(f32)
+        expand_ref[:, at] = parts[j][1].astype(f32)
+    coming.wait()
+    total = jnp.sum(weight[...].astype(f32) * expand_ref[...], axis=1, keepdims=True)
+    gain_out[...] = total / gain_ref[...]
+
+
+def last_wide(place, index, parts, gain, w_expand, after):
+    _, rows, tile = parts[0].shape
+    hidden = PLANE * tile
+    return call(
+        last_wide_kernel,
+        "last_wide",
+        [place, index, *parts, gain, (w_expand,)],
+        [shape_of((rows, hidden), f32)] * 2 + [shape_of((rows, 1), f32)],
+        scratch=[pltpu.VMEM((rows, hidden), bf16)],
+        copies=1,
+        after=after,
+        cost_us=2.0,
+    )
+
+
+def on_plane(
+    segment,
+    memory,
+    compressed,
+    document_labels,
+    memory_filled_count,
+    norm_gain,
+    w_query,
+    w_key,
+    w_value,
+    w_output,
+    ffn_gain,
+    w_expand,
+    w_reduce,
+    w_compress,
+    result_cotangent,
+    compressed_cotangent,
+):
+    _, rows, width = segment.shape
+    blocks = lax.axis_size("blk")
+    block = lax.axis_index("blk")
+    place = lax.axis_index("stream")
+    own = width // blocks
+    seg_len = rows * blocks
+    part_rows = width // (PLANE * blocks)
+    chips = PLANE // 2
+    segment, memory, compressed = segment[0], memory[0], compressed[0]
+    cotangent, comp_cotangent = result_cotangent[0], compressed_cotangent[0]
+    labels, filled = document_labels[0], memory_filled_count[0]
+    gain = norm_gain.reshape(1, width)
+    gain_ffn = ffn_gain.reshape(1, width)
+    block_ref = block.astype(jnp.int32).reshape(1)
+    place_ref = place.astype(jnp.int32).reshape(1)
+    index = place * blocks + block
+    index_ref = index.astype(jnp.int32).reshape(1)
+
+    def along_blk(x, shift):
+        return lax.ppermute(x, "blk", [(i, (i + shift) % blocks) for i in range(blocks)])
+
+    def along_blk_flip(x, flip):
+        return lax.ppermute(x, "blk", [(i, i ^ flip) for i in range(blocks)])
+
+    def in_plane(x, flip):
+        return lax.ppermute(x, "stream", [(i, i ^ flip) for i in range(PLANE)])
+
+    owners = lax.rem(block - jnp.arange(blocks, dtype=jnp.int32) + blocks, blocks)
+    by_owner = labels.reshape(3, blocks, rows).transpose(1, 0, 2)
+    kdoc = by_owner[owners].reshape(blocks, 3 * rows)
+    position = owners[:, None] * rows + jnp.arange(rows, dtype=jnp.int32)[None]
+    first_filled = 2 * seg_len - filled
+    kpos = jnp.concatenate(
+        [
+            jnp.where(position >= first_filled, -1, hidden_slot),
+            jnp.where(position + seg_len >= first_filled, -1, hidden_slot),
+            position,
+        ],
+        axis=1,
+    ).astype(jnp.int32)
+    qdoc = kdoc[:, 2 * rows :].reshape(blocks * rows, 1)
+    qpos = position.reshape(blocks * rows, 1).astype(jnp.int32)
+    marks = (qdoc, qpos, kdoc, kpos)
+
+    def hop(arrays, after):
+        arrays = [gate([x], after)[0] for x in arrays]
+        return arrays, [along_blk(x, 1) for x in arrays]
+
+    weights = (w_query, w_key, w_value)
+    raw = [compressed, memory, segment]
+    arriving = [along_blk(x, 1) for x in raw]
+    pairs = memory.reshape(rows // RATE, RATE * width)
+    projected = [project(block_ref, raw, gain, *weights, width, [])]
+    query = projected[0][1]
+    compress_parts = compress_gradient(
+        place_ref, pairs, in_plane(pairs, 1), comp_cotangent, in_plane(comp_cotangent, 1), [query]
+    )
+    raw, arriving = hop(arriving, [compress_parts[0]])
+    projected.append(raw)
+    cots = [cotangent, in_plane(cotangent, 1)]
+    for j in range(1, chips):
+        cots.append(in_plane(cotangent, 2 * j))
+        cots.append(in_plane(cots[-1], 1))
+    later = []
+    for k in range(2, blocks - 1):
+        raw, arriving = hop(arriving, [query])
+        later.append(raw)
+    compress_parts = [compress_parts[0], *gate(compress_parts[1:], raw)]
+    compress_parts = [compress_parts[0]] + [
+        in_plane(compress_parts[j], 2 * j) for j in range(1, chips)
+    ]
+    projected[1:] = [
+        project(block_ref, rows3, gain, *weights, own, raw) for rows3 in projected[1:] + later
+    ]
+    keys, values = ([p[i] for p in projected] for i in (2, 3))
+    partial = attend(query, keys, values, marks, [])
+    *last, attended, middle, normed_ffn = finish(
+        blocks - 1,
+        block_ref,
+        arriving,
+        gain,
+        *weights,
+        own,
+        query,
+        partial,
+        marks,
+        segment,
+        w_output,
+        gain_ffn,
+        cots[2:],
+    )
+    projected.append(last)
+    normed, queries, keys, values = ([p[i] for p in projected] for i in range(4))
+
+    nfs = [normed_ffn, in_plane(normed_ffn, 1)]
+    for j in range(1, chips - 1):
+        nfs.append(in_plane(normed_ffn, 2 * j))
+        nfs.append(in_plane(nfs[-1], 1))
+    new_compressed = compress(pairs, w_compress, [normed_ffn, *compress_parts[1:]])
+    compress_parts = chip_add(block_ref, blocks, compress_parts, [new_compressed])
+    compress_parts = [compress_parts[0]] + [
+        along_blk_flip(compress_parts[k], k) for k in range(1, blocks)
+    ]
+    *both, res, dn, send = feed(
+        place_ref,
+        normed_ffn,
+        nfs[1],
+        cotangent,
+        cots[1],
+        w_expand,
+        w_reduce,
+        [new_compressed] + nfs[2:5:2],
+    )
+    sent = in_plane(send, 1)
+    both = [both[0], in_plane(both[1], 2), in_plane(both[2], 4), both[3]]
+    result, d_middle, d_branch, *d_attended = leave(
+        block_ref,
+        blocks,
+        res,
+        dn,
+        sent,
+        middle,
+        cotangent,
+        gain_ffn,
+        w_output,
+        nfs[3:6],
+    )
+    grads = [d_attended[0]] + [along_blk(d_attended[k], k) for k in range(1, blocks)]
+    output_keep, output_give = output_gradient(
+        place_ref, attended, d_branch, blocks * part_rows, both[1:3] + grads[1:3]
+    )
+    both[3], diagonal = gate([both[3], normed_ffn], grads[1:])
+    both[3] = in_plane(both[3], 6)
+    nfs.append(in_plane(diagonal, 6))
+    nfs.append(in_plane(nfs[-1], 1))
+    *pieces, dk, dv = attend_back(
+        block_ref, queries, grads, keys, values, marks, [output_keep]
+    )
+    arrived = [pieces[0]] + [along_blk(pieces[k], -k) for k in range(1, blocks)]
+    qkv_keep, qkv_give = heads_gradient(
+        place_ref, normed, pieces, dk, dv, blocks * part_rows, [nfs[6], *compress_parts[1:]]
+    )
+    (output_give,) = gate([output_give], [qkv_keep])
+    part, *moved = plane_gradients(block_ref, cots, nfs, both, blocks, part_rows, [qkv_keep])
+    four = pair_add(
+        place_ref,
+        qkv_keep,
+        in_plane(qkv_give, 1),
+        output_keep,
+        in_plane(output_give, 1),
+        [*moved, *arrived[1:]],
+    )
+    before = four[0]
+    for k in range(2, blocks):
+        for i in range(2):
+            moved[i] = ring_add(block_ref, i, k, along_blk(moved[i], 1), part, [before])
+            before = moved[i]
+    four = [four[0]] + [in_plane(four[j], 2 * j) for j in range(1, chips)]
+    grad_segment = segment_gradient(
+        block_ref, arrived, *weights, segment, gain, d_middle, [before]
+    )
+    parts = chip_add(block_ref, blocks, four, [grad_segment])
+    parts = [parts[0]] + [along_blk_flip(parts[k], k) for k in range(1, blocks)]
+    wide = spread(
+        place_ref, block_ref, [along_blk(x, 1) for x in moved], part, [parts[0]]
+    )
+    wide = [wide[0]] + [in_plane(wide[j], j) for j in range(1, PLANE)]
+
+    def mine(x):
+        return lax.dynamic_slice_in_dim(x, index * part_rows, part_rows, 0).reshape(-1, 1)
+
+    grad_compress = sum(x.astype(f32) for x in compress_parts)
+    grad_query, grad_key, grad_value, grad_output, grad_norm_gain = last_heads(
+        block_ref, index_ref, parts, mine(norm_gain), *weights, [grad_segment]
+    )
+    grad_expand, reduce_turned, grad_ffn_gain = last_wide(
+        place_ref, index_ref, wide, mine(ffn_gain), w_expand, [grad_query]
+    )
+    return (
+        result[None],
+        new_compressed[None],
+        grad_segment[None],
+        grad_norm_gain.reshape(-1),
+        grad_query,
+        grad_key,
+        grad_value,
+        grad_output,
+        grad_ffn_gain.reshape(-1),
+        grad_expand,
+        reduce_turned.T,
+        grad_compress,
+    )
 
 
 def layer_norm(rows_in, gain):
@@ -22,7 +1247,7 @@
     return jax.nn.gelu(values_in, approximate=False)
 
 
-def on_device(
+def on_any(
     segment,
     memory,
     compressed,
@@ -227,38 +1452,21 @@
 
 
 def solution(mesh):
+    tokens = P("stream", "blk", None)
+    both = ("stream", "blk")
     in_specs = (
-        P("stream", "blk", None),
-        P("stream", "blk", None),
-        P("stream", "blk", None),
-        P("stream", None, None),
-        P("stream"),
-        P(),
-        P(),
-        P(),
-        P(),
-        P(),
-        P(),
-        P(),
-        P(),
-        P(),
-        P("stream", "blk", None),
-        P("stream", "blk", None),
+        (tokens,) * 3
+        + (P("stream", None, None), P("stream"))
+        + (P(),) * 9
+        + (tokens,) * 2
     )
     out_specs = (
-        P("stream", "blk", None),
-        P("stream", "blk", None),
-        P("stream", "blk", None),
-        P(("stream", "blk")),
-        P(("stream", "blk"), None),
-        P(("stream", "blk"), None),
-        P(("stream", "blk"), None),
-        P(("stream", "blk"), None),
-        P(("stream", "blk")),
-        P(("stream", "blk"), None),
-        P(None, ("stream", "blk")),
-        P(("stream", "blk"), None),
-    )
+        (tokens,) * 3
+        + (P(both),)
+        + (P(both, None),) * 4
+        + (P(both), P(both, None), P(None, both), P(both, None))
+    )
+    one_plane = mesh.shape["stream"] == PLANE
     return jax.shard_map(
-        on_device, mesh=mesh, in_specs=in_specs, out_specs=out_specs, check_vma=False
-    )
+        on_plane if one_plane else on_any, mesh=mesh, in_specs=in_specs, out_specs=out_specs, check_vma=False
+    )

time: 1850 us -> 235 us (0.13)
  waiting for transfers between devices: 1600 us -> 59.2 us
  matrix products: 101 us -> 0 us
  Pallas kernels: 0 us -> 91.4 us
  starting transfers between devices: 0.41 us -> 53.1 us
  local copies, waits for them, and re-layouts: 63.9 us -> 22 us
  blocking collectives: 41.4 us -> 0 us
    reduce_scatter x6 -> x0, waiting for transfers between devices: 1030 us -> none  [the longest x1 366 us: on_device(): lax.psum_scatter(weight_grads[6], ('stream', 'blk'), scatter_dimension=0,...]
    unnamed x12 -> x0, waiting for transfers between devices: 456 us -> none
    all_gather x2 -> x0, waiting for transfers between devices: 118 us -> none  [the longest x1 59.3 us: on_device(): lax.all_gather(keys, 'blk', axis=0, tiled=True)]
    dot_general x26 -> x0, matrix products: 101 us -> none  [the longest x1 11 us: on_device(): jnp.einsum('srd,srf->df', result_cotangent, activated, preferred_element_...]
    pallas_call x0 -> x33, Pallas kernels: none -> 91.4 us  [the longest x24 91.4 us: call(): pl.pallas_call(body, grid=(1,), in_specs=in_specs, out_specs=[ANY if isin...]
    ppermute x0 -> x62, waiting for transfers between devices: none -> 59.2 us  [the longest x21 35.3 us: along_blk(): lax.ppermute(x, 'blk', [(i, (i + shift) % blocks) for i in range(blocks)])]
    ppermute x0 -> x62, starting transfers between devices: none -> 53.1 us  [the longest x35 26.6 us: in_plane(): return lax.ppermute(x, 'stream', [(i, i ^ flip) for i in range(PLANE)])]
    unnamed x1 -> x0, blocking collectives: 41.4 us -> none
  transfers between devices with their start and end apart: 10 -> 62, of which waited for: 10 -> 22; matrix products, arithmetic and copies ran while one was open for 6% -> 1% of each run, Pallas kernels for 0% -> 32%
where the time goes in v1:
time: 235 us; the launch traced here: 230 us
  Pallas kernels  91.4 us (39%)
  waiting for transfers between devices  59.2 us (25%)
  starting transfers between devices  53.1 us (23%)
  local copies, waits for them, and re-layouts  22 us (9%)
  between operations  2.43 us (1%)
    pallas_call x24, Pallas kernels, call(): pl.pallas_call(body, grid=(1,), in_specs=in_specs, out_specs=[ANY if isin...  91.4 us
    ppermute x21, waiting for transfers between devices, along_blk(): lax.ppermute(x, 'blk', [(i, (i + shift) % blocks) for i in range(blocks)])  35.3 us
    ppermute x35, starting transfers between devices, in_plane(): return lax.ppermute(x, 'stream', [(i, i ^ flip) for i in range(PLANE)])  26.6 us
    ppermute x35, waiting for transfers between devices, in_plane(): return lax.ppermute(x, 'stream', [(i, i ^ flip) for i in range(PLANE)])  22 us
    unnamed x124, local copies, waits for them, and re-layouts  19.7 us
    ppermute x21, starting transfers between devices, along_blk(): lax.ppermute(x, 'blk', [(i, (i + shift) % blocks) for i in range(blocks)])  18.1 us
    ppermute x6, starting transfers between devices, along_blk_flip(): return lax.ppermute(x, 'blk', [(i, i ^ flip) for i in range(blocks)])  8.5 us
  transfers between devices with their start and end apart: 62, of which 22 were waited for; matrix products, arithmetic and copies ran while one was open for 1% of the time, Pallas kernels for 32%

profile of v1, /device:TPU:0, one launch (start us, length us, event | category | flops | bytes accessed | tf_op | source)
XLA Modules:
  0.0 230.3 jit_solution(2150786589222935142)
XLA Ops:
  2.3 3.0 %collective-permute-start.8 = (bf16[128,1024]{1,0:T(8,128)(2,1)}, bf16[128,1024]{1,0:T(8,128)(2,1)}, u32[]{:S(2)}, u32[]{:S(2)}) collective-permute-start(bf16[128,1024]{1,0:T(8,128)(2,1)} %bitcast.40), channel_id=1, source_target_pairs={{0,1},{1,2},{2,3},{3,0},{4,5},{5,6},{6,7},{7,4},{8,9},{9,10},{10,1... | collective-permute-start | bytes 786440 | tf_op jit(solution)/shard_map/ppermute | solution.py:1064
  12.2 5.1 %project.3 = (bf16[384,1024]{1,0:T(8,128)(2,1)}, bf16[128,1024]{1,0:T(8,128)(2,1)}, bf16[384,1024]{1,0:T(8,128)(2,1)}, bf16[384,1024]{1,0:T(8,128)(2,1)}) custom-call(s32[1]{0:T(128)} %bitcast.refs_0_.refs_1_, bf16[128,1024]{1,0:T(8,128)(2,1)} %bitcast.60, bf16[128,1024]{1,0:T(8,128)(2,1)} %bitcast.58, bf16[128,1024]{1,0:T(8,128)(2,1)} %bitcast.41, ...), custom_call_target="tpu_custom_call" | custom-call | flops 50000000 | tf_op jit(solution)/shard_map/project/pallas_call | solution.py:76
  21.0 4.9 %collective-permute-done.refs_0_ = bf16[128,1024]{1,0:T(8,128)(2,1)S(1)} collective-permute-done((bf16[128,1024]{1,0:T(8,128)(2,1)}, bf16[128,1024]{1,0:T(8,128)(2,1)S(1)}, u32[]{:S(2)}, u32[]{:S(2)}) %collective-permute-start) | collective-permute-done | bytes 262176 | tf_op jit(solution)/shard_map/ppermute | solution.py:1064
  28.1 3.5 %collective-permute-done.9.refs_0_ = bf16[128,1024]{1,0:T(8,128)(2,1)S(1)} collective-permute-done((bf16[128,1024]{1,0:T(8,128)(2,1)}, bf16[128,1024]{1,0:T(8,128)(2,1)S(1)}, u32[]{:S(2)}, u32[]{:S(2)}) %collective-permute-start.9) | collective-permute-done | bytes 262176 | tf_op jit(solution)/shard_map/ppermute | solution.py:1064
  33.1 4.1 %collective-permute-done.6.refs_0_ = bf16[128,1024]{1,0:T(8,128)(2,1)S(1)} collective-permute-done((bf16[128,1024]{1,0:T(8,128)(2,1)}, bf16[128,1024]{1,0:T(8,128)(2,1)S(1)}, u32[]{:S(2)}, u32[]{:S(2)}) %collective-permute-start.6) | collective-permute-done | bytes 262176 | tf_op jit(solution)/shard_map/ppermute | solution.py:1064
  37.9 4.9 %collective-permute-done.3.refs_0_ = bf16[128,1024]{1,0:T(8,128)(2,1)S(1)} collective-permute-done((bf16[128,1024]{1,0:T(8,128)(2,1)}, bf16[128,1024]{1,0:T(8,128)(2,1)S(1)}, u32[]{:S(2)}, u32[]{:S(2)}) %collective-permute-start.3) | collective-permute-done | bytes 262176 | tf_op jit(solution)/shard_map/ppermute | solution.py:1064
  50.8 4.9 %project.5 = (bf16[384,1024]{1,0:T(8,128)(2,1)}, bf16[128,256]{1,0:T(8,128)(2,1)}, bf16[384,1024]{1,0:T(8,128)(2,1)}, bf16[384,1024]{1,0:T(8,128)(2,1)}) custom-call(s32[1]{0:T(128)} %bitcast.refs_0_.refs_1_, bf16[128,1024]{1,0:T(8,128)(2,1)} %gate.10.refs_8_.refs_1_.refs_3_, bf16[128,1024]{1,0:T(8,128)(2,1)} %gate.12.refs_9_.refs_2_.refs_4_, ...), custom_call_target="tpu_custom_call" | custom-call | flops 50000000 | tf_op jit(solution)/shard_map/project/pallas_call | solution.py:76
  55.8 4.9 %project.4 = (bf16[384,1024]{1,0:T(8,128)(2,1)}, bf16[128,256]{1,0:T(8,128)(2,1)}, bf16[384,1024]{1,0:T(8,128)(2,1)}, bf16[384,1024]{1,0:T(8,128)(2,1)}) custom-call(s32[1]{0:T(128)} %bitcast.refs_0_.refs_1_, bf16[128,1024]{1,0:T(8,128)(2,1)} %gate.9.refs_1_, bf16[128,1024]{1,0:T(8,128)(2,1)} %gate.11.refs_2_, bf16[128,1024]{1,0:T(8,128)(2,1)} %gate.13.refs_3_, ...), custom_call_target="tpu_custom_call" | custom-call | flops 50000000 | tf_op jit(solution)/shard_map/project/pallas_call | solution.py:76
  60.7 5.9 %attend.1 = (f32[128,1024]{1,0:T(8,128)S(1)}, f32[128,128]{1,0:T(8,128)S(1)}) custom-call(s32[512,1]{1,0:T(8,128)S(1)} %copy.54.refs_0_.refs_11_.refs_1_, s32[512,1]{1,0:T(8,128)S(1)} %copy.55.refs_1_.refs_12_.refs_2_, s32[4,384]{1,0:T(4,128)S(1)} %bitcast.45, s32[4,384]{1,0:T(4,128)S(1)} %pad_add_fusion.refs_3_.refs_14_.refs_4_, ...), custom_call_target="tpu_custom_call" | custom-call | flops 50000000 | tf_op jit(solution)/shard_map/attend/pallas_call | solution.py:76
  68.0 9.3 %finish.1 = (bf16[384,1024]{1,0:T(8,128)(2,1)}, bf16[128,256]{1,0:T(8,128)(2,1)}, bf16[384,1024]{1,0:T(8,128)(2,1)}, bf16[384,1024]{1,0:T(8,128)(2,1)}, bf16[128...) custom-call(s32[1]{0:T(128)} %bitcast.refs_0_.refs_1_, bf16[128,1024]{1,0:T(8,128)(2,1)} %copy-done.60, ...), custom_call_target="tpu_custom_call" | custom-call | flops 4499999744 | tf_op jit(solution)/shard_map/finish/pallas_call | solution.py:76
  82.6 3.2 %compress.1.refs_7_.refs_5_ = bf16[64,1024]{1,0:T(8,128)(2,1)} custom-call(bf16[64,2048]{1,0:T(8,128)(2,1)S(1)} %reshape_squeeze.6.refs_1_.refs_0_, bf16[2048,1024]{1,0:T(8,128)(2,1)} %refs_1_.1, bf16[128,1024]{1,0:T(8,128)(2,1)S(1)} %get-tuple-element.107.refs_2_.refs_1_.refs_9_, bf16[256,1024]{1,0:T(8,128)(2,1)S(1)} %collective-permute-done.19.refs_3_.refs_2_, ...), custom_call_target="tpu_custom_call" | custom-call | flops 1600000000 | tf_op jit(solution)/shard_map/compress/pallas_call | solution.py:76
  85.9 2.3 collective-permute-done.22.refs_8_.refs_11_
  90.3 7.3 %feed.1 = (bf16[2,256,512]{2,1,0:T(8,128)(2,1)}, bf16[2,256,512]{2,1,0:T(8,128)(2,1)}, bf16[2,256,512]{2,1,0:T(8,128)(2,1)}, bf16[2,256,512]{2,1,0:T(8,128)(2,1)...) custom-call(s32[1]{0:T(128)} %bitcast.1.refs_0_, ...), custom_call_target="tpu_custom_call" | custom-call | flops 4000000000 | tf_op jit(solution)/shard_map/feed/pallas_call | solution.py:76
  101.8 3.8 %leave.1 = (bf16[128,1024]{1,0:T(8,128)(2,1)}, f32[128,1024]{1,0:T(8,128)}, bf16[128,1024]{1,0:T(8,128)(2,1)}, bf16[128,256]{1,0:T(8,128)(2,1)S(1)}, bf16[128,25...) custom-call(s32[1]{0:T(128)} %bitcast.refs_0_.refs_1_, ...), custom_call_target="tpu_custom_call" | custom-call | flops 1900000000 | tf_op jit(solution)/shard_map/leave/pallas_call | solution.py:76
  107.2 2.1 collective-permute-start.28
  109.3 2.4 %collective-permute-start.29 = (bf16[128,256]{1,0:T(8,128)(2,1)S(1)}, bf16[128,256]{1,0:T(8,128)(2,1)S(1)}, u32[]{:S(2)}, u32[]{:S(2)}) collective-permute-start(bf16[128,256]{1,0:T(8,128)(2,1)S(1)} %get-tuple-element.122), channel_id=1, source_target_pairs={{0,3},{1,0},{2,1},{3,2},{4,7},{5,4},{6,5},{7,6},{8,11},{9,8},{10,9... | collective-permute-start | bytes 196616 | tf_op jit(solution)/shard_map/ppermute | solution.py:1064
  115.6 2.9 %collective-permute-start.40 = (bf16[64,1024]{1,0:T(8,128)(2,1)S(1)}, bf16[64,1024]{1,0:T(8,128)(2,1)S(1)}, u32[]{:S(2)}, u32[]{:S(2)}) collective-permute-start(bf16[64,1024]{1,0:T(8,128)(2,1)S(1)} %get-tuple-element.150), channel_id=1, source_target_pairs={{0,3},{1,2},{2,1},{3,0},{4,7},{5,6},{6,5},{7,4},{8,11},{9,10},{10,... | collective-permute-start | bytes 393224 | tf_op jit(solution)/shard_map/ppermute | solution.py:1067
  119.9 2.9 %output_gradient.1 = (bf16[4,128,1024]{2,1,0:T(8,128)(2,1)}, bf16[4,128,1024]{2,1,0:T(8,128)(2,1)}) custom-call(s32[1]{0:T(128)} %bitcast.1.refs_0_, bf16[128,1024]{1,0:T(8,128)(2,1)} %get-tuple-element.128.refs_1_, bf16[128,1024]{1,0:T(8,128)(2,1)} %get-tuple-element.129.refs_2_, bf16[2,256,512]{2,1,0:T(8,128)(2,1)S(1)} %collective-permute-done.30.refs_3_.refs_18_, ...), custom_call_target="tpu_custom_call" | custom-call | flops 1400000000 | tf_op jit(solution)/shard_map/output_gradient/pallas_call | solution.py:76
  124.1 11.4 %attend_back.1 = (bf16[128,768]{1,0:T(8,128)(2,1)}, bf16[128,768]{1,0:T(8,128)(2,1)}, bf16[128,768]{1,0:T(8,128)(2,1)}, bf16[128,768]{1,0:T(8,128)(2,1)}, bf16[4...) custom-call(s32[1]{0:T(128)} %bitcast.refs_0_.refs_1_, s32[512,1]{1,0:T(8,128)S(1)} %copy.54.refs_0_.refs_11_.refs_1_, ...), custom_call_target="tpu_custom_call" | custom-call | flops 2000000000 | tf_op jit(solution)/shard_map/attend_back/pallas_call | solution.py:76
  135.6 8.7 %heads_gradient.1 = (bf16[4,128,768]{2,1,0:T(8,128)(2,1)}, bf16[4,128,768]{2,1,0:T(8,128)(2,1)}) custom-call(s32[1]{0:T(128)} %bitcast.1.refs_0_, bf16[128,768]{1,0:T(8,128)(2,1)} %get-tuple-element.133.refs_1_, bf16[128,768]{1,0:T(8,128)(2,1)} %get-tuple-element.134.refs_2_, bf16[128,768]{1,0:T(8,128)(2,1)} %get-tuple-element.135.refs_3_, ...), custom_call_target="tpu_custom_call" | custom-call | flops 50000000 | tf_op jit(solution)/shard_map/heads_gradient/pallas_call | solution.py:76
  150.6 11.3 %collective-permute-done.37.refs_20_ = bf16[2,256,512]{2,1,0:T(8,128)(2,1)S(1)} collective-permute-done((bf16[2,256,512]{2,1,0:T(8,128)(2,1)S(1)}, bf16[2,256,512]{2,1,0:T(8,128)(2,1)S(1)}, u32[]{:S(2)}, u32[]{:S(2)}) %collective-permute-start.37) | collective-permute-done | bytes 524320 | tf_op jit(solution)/shard_map/ppermute | solution.py:1070
  162.7 6.0 %plane_gradients.1 = (bf16[4,2,8,32,512]{4,3,2,1,0:T(8,128)(2,1)}, bf16[8,32,512]{2,1,0:T(8,128)(2,1)S(1)}, bf16[8,32,512]{2,1,0:T(8,128)(2,1)S(1)}) custom-call(s32[1]{0:T(128)} %bitcast.refs_0_.refs_1_, bf16[128,1024]{1,0:T(8,128)(2,1)} %bitcast.34, bf16[128,1024]{1,0:T(8,128)(2,1)} %copy-done.18, bf16[128,1024]{1,0:T(8,128)(2,1)} %copy-done.32, ...), custom_call_target="tpu_custom_call" | custom-call | flops 50000000 | tf_op jit(solution)/shard_map/plane_gradients/pallas_call | solution.py:76
  170.2 2.6 %pair_add.1 = (bf16[128,1792]{1,0:T(8,128)(2,1)}, bf16[128,1792]{1,0:T(8,128)(2,1)}, bf16[128,1792]{1,0:T(8,128)(2,1)}, bf16[128,1792]{1,0:T(8,128)(2,1)}) custom-call(s32[1]{0:T(128)} %bitcast.1.refs_0_, bf16[4,128,768]{2,1,0:T(8,128)(2,1)} %get-tuple-element.151.refs_21_.refs_1_, bf16[4,128,1024]{2,1,0:T(8,128)(2,1)} %get-tuple-element.132.refs_21_.refs_2_, ...), custom_call_target="tpu_custom_call" | custom-call | flops 1500000000 | tf_op jit(solution)/shard_map/pair_add/pallas_call | solution.py:76
  172.8 6.9 %collective-permute-done.42.refs_1_ = bf16[8,32,512]{2,1,0:T(8,128)(2,1)S(1)} collective-permute-done((bf16[8,32,512]{2,1,0:T(8,128)(2,1)S(1)}, bf16[8,32,512]{2,1,0:T(8,128)(2,1)S(1)}, u32[]{:S(2)}, u32[]{:S(2)}) %collective-permute-start.42) | collective-permute-done | bytes 262176 | tf_op jit(solution)/shard_map/ppermute | solution.py:1064
  181.9 2.5 %collective-permute-done.41.refs_1_ = bf16[8,32,512]{2,1,0:T(8,128)(2,1)S(1)} collective-permute-done((bf16[8,32,512]{2,1,0:T(8,128)(2,1)S(1)}, bf16[8,32,512]{2,1,0:T(8,128)(2,1)S(1)}, u32[]{:S(2)}, u32[]{:S(2)}) %collective-permute-start.41) | collective-permute-done | bytes 262176 | tf_op jit(solution)/shard_map/ppermute | solution.py:1064
  189.0 2.6 %collective-permute-done.46.refs_1_ = bf16[8,32,512]{2,1,0:T(8,128)(2,1)S(1)} collective-permute-done((bf16[8,32,512]{2,1,0:T(8,128)(2,1)S(1)}, bf16[8,32,512]{2,1,0:T(8,128)(2,1)S(1)}, u32[]{:S(2)}, u32[]{:S(2)}) %collective-permute-start.46) | collective-permute-done | bytes 262176 | tf_op jit(solution)/shard_map/ppermute | solution.py:1064
  192.7 4.5 %collective-permute-done.45.refs_1_ = bf16[8,32,512]{2,1,0:T(8,128)(2,1)S(1)} collective-permute-done((bf16[8,32,512]{2,1,0:T(8,128)(2,1)S(1)}, bf16[8,32,512]{2,1,0:T(8,128)(2,1)S(1)}, u32[]{:S(2)}, u32[]{:S(2)}) %collective-permute-start.45) | collective-permute-done | bytes 262176 | tf_op jit(solution)/shard_map/ppermute | solution.py:1064
  198.6 4.9 %segment_gradient.1.refs_5_.refs_10_ = bf16[128,1024]{1,0:T(8,128)(2,1)} custom-call(s32[1]{0:T(128)} %bitcast.refs_0_.refs_1_, bf16[128,768]{1,0:T(8,128)(2,1)} %get-tuple-element.133.refs_1_, bf16[128,768]{1,0:T(8,128)(2,1)} %copy-done.43, bf16[128,768]{1,0:T(8,128)(2,1)} %copy-done.44, bf16[128,768]{1,0:T(8,128)(2,1)} %copy-done.45, ...), custom_call_target="tpu_custom_call" | custom-call | flops 2400000000 | tf_op jit(solution)/shard_map/segment_gradient/pallas_call | solution.py:76
  203.5 2.5 %collective-permute-done.48.refs_3_ = bf16[128,1792]{1,0:T(8,128)(2,1)S(1)} collective-permute-done((bf16[128,1792]{1,0:T(8,128)(2,1)}, bf16[128,1792]{1,0:T(8,128)(2,1)S(1)}, u32[]{:S(2)}, u32[]{:S(2)}) %collective-permute-start.48) | collective-permute-done | bytes 458784 | tf_op jit(solution)/shard_map/ppermute | solution.py:1070
  209.0 4.0 %collective-permute-start.51 = (bf16[32,1792]{1,0:T(8,128)(2,1)S(1)}, bf16[32,1792]{1,0:T(8,128)(2,1)S(1)}, u32[]{:S(2)}, u32[]{:S(2)}) collective-permute-start(bf16[32,1792]{1,0:T(8,128)(2,1)S(1)} %get-tuple-element.163), channel_id=1, source_target_pairs={{0,2},{1,3},{2,0},{3,1},{4,6},{5,7},{6,4},{7,5},{8,10},{9,11},{10,... | collective-permute-start | bytes 344072 | tf_op jit(solution)/shard_map/ppermute | solution.py:1067
  222.9 1.7 last_heads.1
  227.5 1.9 last_wide.1
  (267 shorter events, 79.1 us)
Async XLA Ops:
  2.3 17.4 %collective-permute-start.8 = (bf16[128,1024]{1,0:T(8,128)(2,1)}, bf16[128,1024]{1,0:T(8,128)(2,1)}, u32[]{:S(2)}, u32[]{:S(2)}) collective-permute-start(bf16[128,1024]{1,0:T(8,128)(2,1)} %bitcast.40), channel_id=1, source_target_pairs={{0,1},{1,2},{2,3},{3,0},{4,5},{5,6},{6,7},{7,4},{8,9},{9,10},{10,1... | collective-permute-start | bytes 786440 | tf_op jit(solution)/shard_map/ppermute | solution.py:1064
  5.3 15.0 %collective-permute-start.5 = (bf16[128,1024]{1,0:T(8,128)(2,1)}, bf16[128,1024]{1,0:T(8,128)(2,1)S(1)}, u32[]{:S(2)}, u32[]{:S(2)}) collective-permute-start(bf16[128,1024]{1,0:T(8,128)(2,1)} %bitcast.57), channel_id=1, source_target_pairs={{0,1},{1,2},{2,3},{3,0},{4,5},{5,6},{6,7},{7,4},{8,9},{9,10},{10,1... | collective-permute-start | bytes 786440 | tf_op jit(solution)/shard_map/ppermute | solution.py:1064
  6.9 19.0 %collective-permute-start = (bf16[128,1024]{1,0:T(8,128)(2,1)}, bf16[128,1024]{1,0:T(8,128)(2,1)S(1)}, u32[]{:S(2)}, u32[]{:S(2)}) collective-permute-start(bf16[128,1024]{1,0:T(8,128)(2,1)} %bitcast.59), channel_id=1, source_target_pairs={{0,1},{1,2},{2,3},{3,0},{4,5},{5,6},{6,7},{7,4},{8,9},{9,10},{10,1... | collective-permute-start | bytes 786440 | tf_op jit(solution)/shard_map/ppermute | solution.py:1064
  8.4 18.1 %collective-permute-start.11 = (bf16[128,1024]{1,0:T(8,128)(2,1)}, bf16[128,1024]{1,0:T(8,128)(2,1)S(1)}, u32[]{:S(2)}, u32[]{:S(2)}) collective-permute-start(bf16[128,1024]{1,0:T(8,128)(2,1)} %bitcast.32), channel_id=1, source_target_pairs={{0,8},{4,12},{8,0},{12,4},{16,24},{20,28},{24,16},{28,20},{1,9},{5... | collective-permute-start | bytes 786440 | tf_op jit(solution)/shard_map/ppermute | solution.py:1070
  9.9 17.5 %collective-permute-start.13 = (bf16[128,1024]{1,0:T(8,128)(2,1)}, bf16[128,1024]{1,0:T(8,128)(2,1)S(1)}, u32[]{:S(2)}, u32[]{:S(2)}) collective-permute-start(bf16[128,1024]{1,0:T(8,128)(2,1)} %bitcast.33), channel_id=1, source_target_pairs={{0,16},{4,20},{8,24},{12,28},{16,0},{20,4},{24,8},{28,12},{1,17},{... | collective-permute-start | bytes 786440 | tf_op jit(solution)/shard_map/ppermute | solution.py:1070
  26.6 16.2 %collective-permute-start.3 = (bf16[128,1024]{1,0:T(8,128)(2,1)}, bf16[128,1024]{1,0:T(8,128)(2,1)S(1)}, u32[]{:S(2)}, u32[]{:S(2)}) collective-permute-start(bf16[128,1024]{1,0:T(8,128)(2,1)} %gate.9.refs_1_), channel_id=1, source_target_pairs={{0,1},{1,2},{2,3},{3,0},{4,5},{5,6},{6,7},{7,4},{8,9},{9,10},{10,1... | collective-permute-start | bytes 786440 | tf_op jit(solution)/shard_map/ppermute | solution.py:1064
  27.5 16.0 %collective-permute-start.12 = (bf16[128,1024]{1,0:T(8,128)(2,1)S(1)}, bf16[128,1024]{1,0:T(8,128)(2,1)S(1)}, u32[]{:S(2)}, u32[]{:S(2)}) collective-permute-start(bf16[128,1024]{1,0:T(8,128)(2,1)S(1)} %collective-permute-done.11.refs_18_.refs_3_), channel_id=1, source_target_pairs={{0,4},{4,0},{8,12},{12,8},{16,20},{20,16},{24,28},{28,24},{1,5},{5... | collective-permute-start | bytes 786440 | tf_op jit(solution)/shard_map/ppermute | solution.py:1070
  27.6 20.2 %collective-permute-start.14 = (bf16[128,1024]{1,0:T(8,128)(2,1)S(1)}, bf16[128,1024]{1,0:T(8,128)(2,1)}, u32[]{:S(2)}, u32[]{:S(2)}) collective-permute-start(bf16[128,1024]{1,0:T(8,128)(2,1)S(1)} %collective-permute-done.13.refs_20_.refs_5_), channel_id=1, source_target_pairs={{0,4},{4,0},{8,12},{12,8},{16,20},{20,16},{24,28},{28,24},{1,5},{5... | collective-permute-start | bytes 786440 | tf_op jit(solution)/shard_map/ppermute | solution.py:1070
  31.6 17.7 %collective-permute-start.16 = (bf16[128,1024]{1,0:T(8,128)(2,1)S(1)}, bf16[128,1024]{1,0:T(8,128)(2,1)}, u32[]{:S(2)}, u32[]{:S(2)}) collective-permute-start(bf16[128,1024]{1,0:T(8,128)(2,1)S(1)} %collective-permute-done.15.refs_22_.refs_7_), channel_id=1, source_target_pairs={{0,4},{4,0},{8,12},{12,8},{16,20},{20,16},{24,28},{28,24},{1,5},{5... | collective-permute-start | bytes 786440 | tf_op jit(solution)/shard_map/ppermute | solution.py:1070
  37.2 29.4 %collective-permute-start.10 = (bf16[128,1024]{1,0:T(8,128)(2,1)}, bf16[128,1024]{1,0:T(8,128)(2,1)S(1)}, u32[]{:S(2)}, u32[]{:S(2)}) collective-permute-start(bf16[128,1024]{1,0:T(8,128)(2,1)} %gate.14.refs_10_.refs_3_.refs_5_), channel_id=1, source_target_pairs={{0,1},{1,2},{2,3},{3,0},{4,5},{5,6},{6,7},{7,4},{8,9},{9,10},{10,1... | collective-permute-start | bytes 786440 | tf_op jit(solution)/shard_map/ppermute | solution.py:1064
  42.8 23.9 %collective-permute-start.7 = (bf16[128,1024]{1,0:T(8,128)(2,1)}, bf16[128,1024]{1,0:T(8,128)(2,1)S(1)}, u32[]{:S(2)}, u32[]{:S(2)}) collective-permute-start(bf16[128,1024]{1,0:T(8,128)(2,1)} %gate.12.refs_9_.refs_2_.refs_4_), channel_id=1, source_target_pairs={{0,1},{1,2},{2,3},{3,0},{4,5},{5,6},{6,7},{7,4},{8,9},{9,10},{10,1... | collective-permute-start | bytes 786440 | tf_op jit(solution)/shard_map/ppermute | solution.py:1064
  43.5 23.8 %collective-permute-start.4 = (bf16[128,1024]{1,0:T(8,128)(2,1)}, bf16[128,1024]{1,0:T(8,128)(2,1)S(1)}, u32[]{:S(2)}, u32[]{:S(2)}) collective-permute-start(bf16[128,1024]{1,0:T(8,128)(2,1)} %gate.10.refs_8_.refs_1_.refs_3_), channel_id=1, source_target_pairs={{0,1},{1,2},{2,3},{3,0},{4,5},{5,6},{6,7},{7,4},{8,9},{9,10},{10,1... | collective-permute-start | bytes 786440 | tf_op jit(solution)/shard_map/ppermute | solution.py:1064
  47.8 31.9 %collective-permute-start.19 = (bf16[256,1024]{1,0:T(8,128)(2,1)}, bf16[256,1024]{1,0:T(8,128)(2,1)S(1)}, u32[]{:S(2)}, u32[]{:S(2)}) collective-permute-start(bf16[256,1024]{1,0:T(8,128)(2,1)} %get-tuple-element.111), channel_id=1, source_target_pairs={{0,8},{4,12},{8,0},{12,4},{16,24},{20,28},{24,16},{28,20},{1,9},{5... | collective-permute-start | bytes 1572872 | tf_op jit(solution)/shard_map/ppermute | solution.py:1070
  49.3 31.8 %collective-permute-start.20 = (bf16[256,1024]{1,0:T(8,128)(2,1)}, bf16[256,1024]{1,0:T(8,128)(2,1)S(1)}, u32[]{:S(2)}, u32[]{:S(2)}) collective-permute-start(bf16[256,1024]{1,0:T(8,128)(2,1)} %get-tuple-element.112), channel_id=1, source_target_pairs={{0,16},{4,20},{8,24},{12,28},{16,0},{20,4},{24,8},{28,12},{1,17},{... | collective-permute-start | bytes 1572872 | tf_op jit(solution)/shard_map/ppermute | solution.py:1070
  66.6 19.2 %collective-permute-start.18 = (bf16[128,1024]{1,0:T(8,128)(2,1)S(1)}, bf16[128,1024]{1,0:T(8,128)(2,1)S(1)}, u32[]{:S(2)}, u32[]{:S(2)}) collective-permute-start(bf16[128,1024]{1,0:T(8,128)(2,1)S(1)} %bitcast.36), channel_id=1, source_target_pairs={{0,4},{4,0},{8,12},{12,8},{16,20},{20,16},{24,28},{28,24},{1,5},{5... | collective-permute-start | bytes 786440 | tf_op jit(solution)/shard_map/ppermute | solution.py:1070
  66.7 15.9 %collective-permute-start.21 = (bf16[256,1024]{1,0:T(8,128)(2,1)S(1)}, bf16[256,1024]{1,0:T(8,128)(2,1)S(1)}, u32[]{:S(2)}, u32[]{:S(2)}) collective-permute-start(bf16[256,1024]{1,0:T(8,128)(2,1)S(1)} %copy-done.31), channel_id=1, source_target_pairs={{0,24},{4,28},{8,16},{12,20},{16,8},{20,12},{24,0},{28,4},{1,25},{... | collective-permute-start | bytes 1572872 | tf_op jit(solution)/shard_map/ppermute | solution.py:1070
  97.7 20.7 %collective-permute-start.30 = (bf16[2,256,512]{2,1,0:T(8,128)(2,1)}, bf16[2,256,512]{2,1,0:T(8,128)(2,1)S(1)}, u32[]{:S(2)}, u32[]{:S(2)}) collective-permute-start(bf16[2,256,512]{2,1,0:T(8,128)(2,1)} %get-tuple-element.130), channel_id=1, source_target_pairs={{0,8},{4,12},{8,0},{12,4},{16,24},{20,28},{24,16},{28,20},{1,9},{5... | collective-permute-start | bytes 1572872 | tf_op jit(solution)/shard_map/ppermute | solution.py:1070
  98.3 21.6 %collective-permute-start.31 = (bf16[2,256,512]{2,1,0:T(8,128)(2,1)}, bf16[2,256,512]{2,1,0:T(8,128)(2,1)S(1)}, u32[]{:S(2)}, u32[]{:S(2)}) collective-permute-start(bf16[2,256,512]{2,1,0:T(8,128)(2,1)} %get-tuple-element.131), channel_id=1, source_target_pairs={{0,16},{4,20},{8,24},{12,28},{16,0},{20,4},{24,8},{28,12},{1,17},{... | collective-permute-start | bytes 1572872 | tf_op jit(solution)/shard_map/ppermute | solution.py:1070
  112.9 22.6 %collective-permute-start.38 = (bf16[64,1024]{1,0:T(8,128)(2,1)S(1)}, bf16[64,1024]{1,0:T(8,128)(2,1)S(1)}, u32[]{:S(2)}, u32[]{:S(2)}) collective-permute-start(bf16[64,1024]{1,0:T(8,128)(2,1)S(1)} %get-tuple-element.148), channel_id=1, source_target_pairs={{0,1},{1,0},{2,3},{3,2},{4,5},{5,4},{6,7},{7,6},{8,9},{9,8},{10,11... | collective-permute-start | bytes 393224 | tf_op jit(solution)/shard_map/ppermute | solution.py:1067
  114.5 21.1 %collective-permute-start.39 = (bf16[64,1024]{1,0:T(8,128)(2,1)S(1)}, bf16[64,1024]{1,0:T(8,128)(2,1)S(1)}, u32[]{:S(2)}, u32[]{:S(2)}) collective-permute-start(bf16[64,1024]{1,0:T(8,128)(2,1)S(1)} %get-tuple-element.149), channel_id=1, source_target_pairs={{0,2},{1,3},{2,0},{3,1},{4,6},{5,7},{6,4},{7,5},{8,10},{9,11},{10,... | collective-permute-start | bytes 393224 | tf_op jit(solution)/shard_map/ppermute | solution.py:1067
  115.6 20.0 %collective-permute-start.40 = (bf16[64,1024]{1,0:T(8,128)(2,1)S(1)}, bf16[64,1024]{1,0:T(8,128)(2,1)S(1)}, u32[]{:S(2)}, u32[]{:S(2)}) collective-permute-start(bf16[64,1024]{1,0:T(8,128)(2,1)S(1)} %get-tuple-element.150), channel_id=1, source_target_pairs={{0,3},{1,2},{2,1},{3,0},{4,7},{5,6},{6,5},{7,4},{8,11},{9,10},{10,... | collective-permute-start | bytes 393224 | tf_op jit(solution)/shard_map/ppermute | solution.py:1067
  118.5 17.1 %collective-permute-start.35 = (bf16[128,1024]{1,0:T(8,128)(2,1)}, bf16[128,1024]{1,0:T(8,128)(2,1)S(1)}, u32[]{:S(2)}, u32[]{:S(2)}) collective-permute-start(bf16[128,1024]{1,0:T(8,128)(2,1)} %get-tuple-element.139), channel_id=1, source_target_pairs={{0,24},{4,28},{8,16},{12,20},{16,8},{20,12},{24,0},{28,4},{1,25},{... | collective-permute-start | bytes 786440 | tf_op jit(solution)/shard_map/ppermute | solution.py:1070
  145.5 24.7 %collective-permute-start.44 = (bf16[4,128,1024]{2,1,0:T(8,128)(2,1)}, bf16[4,128,1024]{2,1,0:T(8,128)(2,1)S(1)}, u32[]{:S(2)}, u32[]{:S(2)}) collective-permute-start(bf16[4,128,1024]{2,1,0:T(8,128)(2,1)} %gate.17), channel_id=1, source_target_pairs={{0,4},{4,0},{8,12},{12,8},{16,20},{20,16},{24,28},{28,24},{1,5},{5... | collective-permute-start | bytes 3145736 | tf_op jit(solution)/shard_map/ppermute | solution.py:1070
  146.6 23.6 %collective-permute-start.43 = (bf16[4,128,768]{2,1,0:T(8,128)(2,1)S(1)}, bf16[4,128,768]{2,1,0:T(8,128)(2,1)S(1)}, u32[]{:S(2)}, u32[]{:S(2)}) collective-permute-start(bf16[4,128,768]{2,1,0:T(8,128)(2,1)S(1)} %copy-done.57), channel_id=1, source_target_pairs={{0,4},{4,0},{8,12},{12,8},{16,20},{20,16},{24,28},{28,24},{1,5},{5... | collective-permute-start | bytes 2359304 | tf_op jit(solution)/shard_map/ppermute | solution.py:1070
  146.6 15.2 %collective-permute-start.37 = (bf16[2,256,512]{2,1,0:T(8,128)(2,1)S(1)}, bf16[2,256,512]{2,1,0:T(8,128)(2,1)S(1)}, u32[]{:S(2)}, u32[]{:S(2)}) collective-permute-start(bf16[2,256,512]{2,1,0:T(8,128)(2,1)S(1)} %copy-done.51), channel_id=1, source_target_pairs={{0,24},{4,28},{8,16},{12,20},{16,8},{20,12},{24,0},{28,4},{1,25},{... | collective-permute-start | bytes 1572872 | tf_op jit(solution)/shard_map/ppermute | solution.py:1070
  148.4 20.3 %collective-permute-start.32 = (bf16[128,768]{1,0:T(8,128)(2,1)S(1)}, bf16[128,768]{1,0:T(8,128)(2,1)S(1)}, u32[]{:S(2)}, u32[]{:S(2)}) collective-permute-start(bf16[128,768]{1,0:T(8,128)(2,1)S(1)} %copy-done.55), channel_id=1, source_target_pairs={{0,3},{1,0},{2,1},{3,2},{4,7},{5,4},{6,5},{7,6},{8,11},{9,8},{10,9... | collective-permute-start | bytes 589832 | tf_op jit(solution)/shard_map/ppermute | solution.py:1064
  149.7 19.7 %collective-permute-start.33 = (bf16[128,768]{1,0:T(8,128)(2,1)S(1)}, bf16[128,768]{1,0:T(8,128)(2,1)S(1)}, u32[]{:S(2)}, u32[]{:S(2)}) collective-permute-start(bf16[128,768]{1,0:T(8,128)(2,1)S(1)} %copy-done.54), channel_id=1, source_target_pairs={{0,2},{1,3},{2,0},{3,1},{4,6},{5,7},{6,4},{7,5},{8,10},{9,11},{10,... | collective-permute-start | bytes 589832 | tf_op jit(solution)/shard_map/ppermute | solution.py:1064
  185.4 18.1 %collective-permute-start.47 = (bf16[128,1792]{1,0:T(8,128)(2,1)}, bf16[128,1792]{1,0:T(8,128)(2,1)S(1)}, u32[]{:S(2)}, u32[]{:S(2)}) collective-permute-start(bf16[128,1792]{1,0:T(8,128)(2,1)} %get-tuple-element.158), channel_id=1, source_target_pairs={{0,8},{4,12},{8,0},{12,4},{16,24},{20,28},{24,16},{28,20},{1,9},{5... | collective-permute-start | bytes 1376264 | tf_op jit(solution)/shard_map/ppermute | solution.py:1070
  185.9 20.1 %collective-permute-start.48 = (bf16[128,1792]{1,0:T(8,128)(2,1)}, bf16[128,1792]{1,0:T(8,128)(2,1)S(1)}, u32[]{:S(2)}, u32[]{:S(2)}) collective-permute-start(bf16[128,1792]{1,0:T(8,128)(2,1)} %get-tuple-element.159), channel_id=1, source_target_pairs={{0,16},{4,20},{8,24},{12,28},{16,0},{20,4},{24,8},{28,12},{1,17},{... | collective-permute-start | bytes 1376264 | tf_op jit(solution)/shard_map/ppermute | solution.py:1070
  187.5 20.0 %collective-permute-start.49 = (bf16[128,1792]{1,0:T(8,128)(2,1)}, bf16[128,1792]{1,0:T(8,128)(2,1)S(1)}, u32[]{:S(2)}, u32[]{:S(2)}) collective-permute-start(bf16[128,1792]{1,0:T(8,128)(2,1)} %get-tuple-element.160), channel_id=1, source_target_pairs={{0,24},{4,28},{8,16},{12,20},{16,8},{20,12},{24,0},{28,4},{1,25},{... | collective-permute-start | bytes 1376264 | tf_op jit(solution)/shard_map/ppermute | solution.py:1070
  192.7 20.7 %collective-permute-start.53 = (bf16[8,32,512]{2,1,0:T(8,128)(2,1)S(1)}, bf16[8,32,512]{2,1,0:T(8,128)(2,1)S(1)}, u32[]{:S(2)}, u32[]{:S(2)}) collective-permute-start(bf16[8,32,512]{2,1,0:T(8,128)(2,1)S(1)} %ring_add.6.refs_3_), channel_id=1, source_target_pairs={{0,1},{1,2},{2,3},{3,0},{4,5},{5,6},{6,7},{7,4},{8,9},{9,10},{10,1... | collective-permute-start | bytes 786440 | tf_op jit(solution)/shard_map/ppermute | solution.py:1064
  198.3 15.1 %collective-permute-start.54 = (bf16[8,32,512]{2,1,0:T(8,128)(2,1)S(1)}, bf16[8,32,512]{2,1,0:T(8,128)(2,1)S(1)}, u32[]{:S(2)}, u32[]{:S(2)}) collective-permute-start(bf16[8,32,512]{2,1,0:T(8,128)(2,1)S(1)} %ring_add.7.refs_11_), channel_id=1, source_target_pairs={{0,1},{1,2},{2,3},{3,0},{4,5},{5,6},{6,7},{7,4},{8,9},{9,10},{10,1... | collective-permute-start | bytes 786440 | tf_op jit(solution)/shard_map/ppermute | solution.py:1064
  (91 other events, 622.7 us)
